TPU v7x, 32 devices: a whole 2x2x4 slice. The times are simulated.
32 devices in a mesh: groups: 2 (over y), ctx: 4 (over z), mp: 4 (over x, core).
Axes of the slice: x: 2, y: 2, z: 4, core: 2. Of those that a mesh axis runs over, the one named last changes fastest.
Arguments:
- queries: bfloat16 [2048, 4096], P(('groups', 'ctx'), 'mp'), parts along dimension 0, may hold values from -18 to 18
- keyvals: bfloat16 [2048, 512], P(('groups', 'ctx', 'mp')), parts along dimension 0, may hold values from -6 to 6
- segment_ids: int32 [2048], P('groups'), parts along dimension 0, may hold values from 0 to 2, never falling along the last dimension, each value on 1 to 512 neighbouring positions
- residual: bfloat16 [2048, 4096], P(('groups', 'ctx', 'mp')), parts along dimension 0, may hold values from -180 to 180
- out_weight: bfloat16 [4096, 4096], P('mp', 'ctx'), may hold values from -0.375 to 0.375
- lru_weight: bfloat16 [4096, 4096], P('ctx', 'mp'), may hold values from -0.09375 to 0.09375
- conv_weight: float32 [4, 4096], P(None, 'mp'), may hold values from -3 to 3
- gate_decay_w: bfloat16 [16, 256, 256], P('mp'), may hold values from -0.375 to 0.375
- gate_input_w: bfloat16 [16, 256, 256], P('mp'), may hold values from -0.375 to 0.375
- gate_decay_b: float32 [4096], P('mp'), may hold values from -3 to 3
- gate_input_b: float32 [4096], P('mp'), may hold values from -3 to 3
- decay_codes: int32 [4096], P('mp'), may hold values from 0 to 15
- norm_gain: float32 [4096], replicated, may hold values from 0.1 to 1.9
Outputs:
- resid_out: bfloat16 [2048, 4096], P(('groups', 'ctx', 'mp')), parts along dimension 0
- lru_out: bfloat16 [2048, 4096], P(('groups', 'ctx'), 'mp'), parts along dimension 0
There are 2 independent parts, one for each index of `groups`. A program takes and returns all parts, laid end to end along the dimension named above; an argument that names none is the same for every part. Nothing has to cross between parts.
All inputs are finite; a program needn't handle non-finite values.
Results may differ from a plain program's by a relative error of at most 0.017.
Values may be sent and summed in bfloat16 or wider, within the bound.
A program may use at most 64 MiB of HBM per device.

v0:
```python
import math

import jax
import jax.numpy as jnp
from jax import lax
from jax.sharding import PartitionSpec as P

HD = 256
WIN = 2048
CONV = 4
LEVELS = 16
BW = 256


def shifted_2(value, axis, steps):
    count = lax.axis_size(axis)
    initial, last = (max(0, -steps), min(count, count - steps))
    return lax.ppermute(value, axis, [(source, source + steps) for source in range(initial, last)])


def decay_rates():
    levels = jnp.arange(LEVELS, dtype=jnp.float32)
    return 0.006 * jnp.exp(-levels * (math.log(3000.0) / (LEVELS - 1)))


def chain_link(former, latter):
    return (former[0] * latter[0], latter[0] * former[1] + latter[1])


def rms_scaled(values, norm_gain):
    value_f32 = values.astype(jnp.float32)
    inverse = lax.rsqrt(jnp.mean(value_f32 * value_f32, axis=-1, keepdims=True) + 1e-06)
    return (value_f32 * inverse * norm_gain).astype(jnp.bfloat16)


def attend_local(queries, keys_all, allowed):
    rows_here = queries.shape[0]
    heads_here = queries.shape[1] // HD
    query_heads = queries.reshape(rows_here, heads_here, HD)
    score_scale = 1.0 / math.sqrt(HD)
    scores = (
        jnp.einsum("thd,kd->htk", query_heads, keys_all[:, :HD], preferred_element_type=jnp.float32)
        * score_scale
    )
    scores = jnp.where(allowed[None], scores, -1e30)
    row_top = jnp.max(scores, axis=-1, keepdims=True)
    weights = jnp.exp(scores - row_top)
    probs = (weights / jnp.sum(weights, axis=-1, keepdims=True)).astype(jnp.bfloat16)
    gathered = jnp.einsum(
        "htk,kd->thd", probs, keys_all[:, HD:], preferred_element_type=jnp.float32
    )
    return gathered.reshape(rows_here, heads_here * HD).astype(jnp.bfloat16)


def local(
    queries,
    keyvals,
    segment_ids,
    residual,
    out_weight,
    lru_weight,
    conv_weight,
    gate_decay_w,
    gate_input_w,
    gate_decay_b,
    gate_input_b,
    decay_codes,
    norm_gain,
):
    rows_here = queries.shape[0]
    ctx_index = lax.axis_index("ctx")
    back_blocks = WIN // rows_here
    own_kv = lax.all_gather(keyvals, "mp", axis=0, tiled=True)
    earlier = []
    moving = own_kv
    for offset in range(back_blocks):
        moving = shifted_2(moving, "ctx", 1)
        earlier = [moving] + earlier
    keys_all = jnp.concatenate(earlier + [own_kv], axis=0)
    pad_seg = jnp.concatenate([jnp.full((WIN,), -1, jnp.int32), segment_ids])
    query_seg = lax.dynamic_slice_in_dim(segment_ids, ctx_index * rows_here, rows_here)
    key_seg = lax.dynamic_slice_in_dim(
        pad_seg, ctx_index * rows_here, (back_blocks + 1) * rows_here
    )
    query_pos = ctx_index * rows_here + jnp.arange(rows_here, dtype=jnp.int32)
    key_pos = (ctx_index - back_blocks) * rows_here + jnp.arange(
        (back_blocks + 1) * rows_here, dtype=jnp.int32
    )
    distance = query_pos[:, None] - key_pos[None, :]
    allowed = (distance >= 0) & (distance < WIN) & (query_seg[:, None] == key_seg[None, :])
    attended = attend_local(queries, keys_all, allowed)
    head_part = jnp.dot(
        attended,
        lax.all_gather(out_weight, "ctx", axis=1, tiled=True),
        preferred_element_type=jnp.float32,
    )
    summed = lax.psum_scatter(
        head_part.astype(jnp.bfloat16), "mp", scatter_dimension=0, tiled=True
    ).astype(jnp.float32)
    resid_out = (summed + residual.astype(jnp.float32)).astype(jnp.bfloat16)
    normed = lax.all_gather(rms_scaled(resid_out, norm_gain), "mp", axis=0, tiled=True)
    channels = lru_weight.shape[1]
    lru_in = jnp.dot(
        normed,
        lax.all_gather(lru_weight, "ctx", axis=0, tiled=True),
        preferred_element_type=jnp.float32,
    ).astype(jnp.bfloat16)
    rim_rows = shifted_2(lru_in[rows_here - (CONV - 1) :], "ctx", 1)
    extended = jnp.concatenate([rim_rows, lru_in], axis=0)
    ext_seg = lax.dynamic_slice_in_dim(
        pad_seg, ctx_index * rows_here + WIN - (CONV - 1), rows_here + CONV - 1
    )
    conv_acc = jnp.zeros((rows_here, channels), jnp.float32)
    for offset in range(CONV):
        lag_rows = CONV - 1 - offset
        shifted = extended[lag_rows : lag_rows + rows_here].astype(jnp.float32)
        same_doc = (ext_seg[lag_rows : lag_rows + rows_here] == query_seg)[:, None]
        conv_acc = conv_acc + jnp.where(same_doc, conv_weight[offset] * shifted, 0.0)
    conv_out = conv_acc.astype(jnp.bfloat16)
    blocks_here = channels // BW
    grouped = conv_out.reshape(rows_here, blocks_here, BW)
    decay_gate = jax.nn.sigmoid(
        jnp.einsum(
            "tbi,bij->tbj", grouped, gate_decay_w, preferred_element_type=jnp.float32
        ).reshape(rows_here, channels)
        + gate_decay_b
    )
    input_gate = jax.nn.sigmoid(
        jnp.einsum(
            "tbi,bij->tbj", grouped, gate_input_w, preferred_element_type=jnp.float32
        ).reshape(rows_here, channels)
        + gate_input_b
    )
    levels = jnp.arange(LEVELS, dtype=jnp.int32)
    decay_rate = jnp.sum(
        jnp.where(decay_codes[:, None] == levels[None, :], decay_rates()[None, :], 0.0), axis=1
    )
    log_decay = -8.0 * decay_gate * decay_rate
    restart = (query_seg != ext_seg[CONV - 2 : CONV - 2 + rows_here])[:, None]
    keep_factor = jnp.where(restart, 0.0, jnp.exp(log_decay))
    input_scale = jnp.where(restart, 1.0, jnp.sqrt(-jnp.expm1(2.0 * log_decay)))
    driven = input_scale * input_gate * conv_out.astype(jnp.float32)
    cum_keep, local_state = lax.associative_scan(chain_link, (keep_factor, driven), axis=0)
    block_keep = cum_keep[rows_here - 1]
    block_state = local_state[rows_here - 1]

    def relay_turn(turn_index, state_in):
        return shifted_2(block_keep * state_in + block_state, "ctx", 1)

    incoming = lax.fori_loop(0, lax.axis_size("ctx") - 1, relay_turn, jnp.zeros_like(block_state))
    states = local_state + cum_keep * incoming[None, :]
    return (resid_out, states.astype(jnp.bfloat16))


def solution(mesh):
    in_specs = (
        P(("groups", "ctx"), "mp"),
        P(("groups", "ctx", "mp"), None),
        P("groups"),
        P(("groups", "ctx", "mp"), None),
        P("mp", "ctx"),
        P("ctx", "mp"),
        P(None, "mp"),
        P("mp", None, None),
        P("mp", None, None),
        P("mp"),
        P("mp"),
        P("mp"),
        P(),
    )
    out_specs = (P(("groups", "ctx", "mp"), None), P(("groups", "ctx"), "mp"))
    return jax.shard_map(local, mesh=mesh, in_specs=in_specs, out_specs=out_specs, check_vma=False)
```

profile of v0, /device:TPU:0, one launch (start us, length us, event | category | flops | bytes accessed | tf_op | source)
XLA Modules:
  0.0 559.0 jit_solution(5232723126797398906)
XLA Ops:
  8.0 7.4 %all_gather.12 = bf16[256,512]{1,0:T(8,128)(2,1)S(1)} all-gather(bf16[64,512]{1,0:T(8,128)(2,1)} %param.16), channel_id=1, replica_groups=mesh['groups'=2,'ctx'=4,'mp'=4] {'mp'}, dimensions={0}, use_global_device_ids=true | all-gather | bytes 327680 | tf_op jit(solution)/shard_map/all_gather | solution.py:73
  15.4 3.5 collective-permute-start.1
  18.9 9.1 %collective-permute-done.1 = bf16[256,512]{1,0:T(8,128)(2,1)S(1)} collective-permute-done((bf16[256,512]{1,0:T(8,128)(2,1)S(1)}, bf16[256,512]{1,0:T(8,128)(2,1)S(1)}, u32[]{:S(2)}, u32[]{:S(2)}) %collective-permute-start.1) | collective-permute-done | bytes 262176 | tf_op jit(solution)/shard_map/ppermute | solution.py:18
  28.0 8.4 %collective-permute-start.2 = (bf16[256,512]{1,0:T(8,128)(2,1)S(1)}, bf16[256,512]{1,0:T(8,128)(2,1)S(1)}, u32[]{:S(2)}, u32[]{:S(2)}) collective-permute-start(bf16[256,512]{1,0:T(8,128)(2,1)S(1)} %collective-permute-done.1), channel_id=1, source_target_pairs={{0,4},{4,8},{8,12},{1,5},{5,9},{9,13},{2,6},{6,10},{10,14},{3,7},{... | collective-permute-start | bytes 786440 | tf_op jit(solution)/shard_map/ppermute | solution.py:18
  36.5 11.2 %collective-permute-done.2 = bf16[256,512]{1,0:T(8,128)(2,1)S(1)} collective-permute-done((bf16[256,512]{1,0:T(8,128)(2,1)S(1)}, bf16[256,512]{1,0:T(8,128)(2,1)S(1)}, u32[]{:S(2)}, u32[]{:S(2)}) %collective-permute-start.2) | collective-permute-done | bytes 262176 | tf_op jit(solution)/shard_map/ppermute | solution.py:18
  47.7 12.9 %collective-permute-start.3 = (bf16[256,512]{1,0:T(8,128)(2,1)S(1)}, bf16[256,512]{1,0:T(8,128)(2,1)S(1)}, u32[]{:S(2)}, u32[]{:S(2)}) collective-permute-start(bf16[256,512]{1,0:T(8,128)(2,1)S(1)} %collective-permute-done.2), channel_id=1, source_target_pairs={{0,4},{4,8},{8,12},{1,5},{5,9},{9,13},{2,6},{6,10},{10,14},{3,7},{... | collective-permute-start | bytes 786440 | tf_op jit(solution)/shard_map/ppermute | solution.py:18
  60.6 10.3 %collective-permute-done.3 = bf16[256,512]{1,0:T(8,128)(2,1)S(1)} collective-permute-done((bf16[256,512]{1,0:T(8,128)(2,1)S(1)}, bf16[256,512]{1,0:T(8,128)(2,1)S(1)}, u32[]{:S(2)}, u32[]{:S(2)}) %collective-permute-start.3) | collective-permute-done | bytes 262176 | tf_op jit(solution)/shard_map/ppermute | solution.py:18
  70.9 12.6 %collective-permute-start.4 = (bf16[256,512]{1,0:T(8,128)(2,1)S(1)}, bf16[256,512]{1,0:T(8,128)(2,1)S(1)}, u32[]{:S(2)}, u32[]{:S(2)}) collective-permute-start(bf16[256,512]{1,0:T(8,128)(2,1)S(1)} %collective-permute-done.3), channel_id=1, source_target_pairs={{0,4},{4,8},{8,12},{1,5},{5,9},{9,13},{2,6},{6,10},{10,14},{3,7},{... | collective-permute-start | bytes 786440 | tf_op jit(solution)/shard_map/ppermute | solution.py:18
  83.5 9.4 %collective-permute-done.4 = bf16[256,512]{1,0:T(8,128)(2,1)S(1)} collective-permute-done((bf16[256,512]{1,0:T(8,128)(2,1)S(1)}, bf16[256,512]{1,0:T(8,128)(2,1)S(1)}, u32[]{:S(2)}, u32[]{:S(2)}) %collective-permute-start.4) | collective-permute-done | bytes 262176 | tf_op jit(solution)/shard_map/ppermute | solution.py:18
  92.9 9.8 %collective-permute-start.5 = (bf16[256,512]{1,0:T(8,128)(2,1)S(1)}, bf16[256,512]{1,0:T(8,128)(2,1)S(1)}, u32[]{:S(2)}, u32[]{:S(2)}) collective-permute-start(bf16[256,512]{1,0:T(8,128)(2,1)S(1)} %collective-permute-done.4), channel_id=1, source_target_pairs={{0,4},{4,8},{8,12},{1,5},{5,9},{9,13},{2,6},{6,10},{10,14},{3,7},{... | collective-permute-start | bytes 786440 | tf_op jit(solution)/shard_map/ppermute | solution.py:18
  102.8 10.0 %collective-permute-done.5 = bf16[256,512]{1,0:T(8,128)(2,1)S(1)} collective-permute-done((bf16[256,512]{1,0:T(8,128)(2,1)S(1)}, bf16[256,512]{1,0:T(8,128)(2,1)S(1)}, u32[]{:S(2)}, u32[]{:S(2)}) %collective-permute-start.5) | collective-permute-done | bytes 262176 | tf_op jit(solution)/shard_map/ppermute | solution.py:18
  112.8 13.7 %collective-permute-start.6 = (bf16[256,512]{1,0:T(8,128)(2,1)S(1)}, bf16[256,512]{1,0:T(8,128)(2,1)S(1)}, u32[]{:S(2)}, u32[]{:S(2)}) collective-permute-start(bf16[256,512]{1,0:T(8,128)(2,1)S(1)} %collective-permute-done.5), channel_id=1, source_target_pairs={{0,4},{4,8},{8,12},{1,5},{5,9},{9,13},{2,6},{6,10},{10,14},{3,7},{... | collective-permute-start | bytes 786440 | tf_op jit(solution)/shard_map/ppermute | solution.py:18
  126.7 9.3 %collective-permute-done.6 = bf16[256,512]{1,0:T(8,128)(2,1)S(1)} collective-permute-done((bf16[256,512]{1,0:T(8,128)(2,1)S(1)}, bf16[256,512]{1,0:T(8,128)(2,1)S(1)}, u32[]{:S(2)}, u32[]{:S(2)}) %collective-permute-start.6) | collective-permute-done | bytes 262176 | tf_op jit(solution)/shard_map/ppermute | solution.py:18
  136.0 10.9 %collective-permute-start.7 = (bf16[256,512]{1,0:T(8,128)(2,1)S(1)}, bf16[256,512]{1,0:T(8,128)(2,1)S(1)}, u32[]{:S(2)}, u32[]{:S(2)}) collective-permute-start(bf16[256,512]{1,0:T(8,128)(2,1)S(1)} %collective-permute-done.6), channel_id=1, source_target_pairs={{0,4},{4,8},{8,12},{1,5},{5,9},{9,13},{2,6},{6,10},{10,14},{3,7},{... | collective-permute-start | bytes 786440 | tf_op jit(solution)/shard_map/ppermute | solution.py:18
  147.0 10.3 %collective-permute-done.7 = bf16[256,512]{1,0:T(8,128)(2,1)S(1)} collective-permute-done((bf16[256,512]{1,0:T(8,128)(2,1)S(1)}, bf16[256,512]{1,0:T(8,128)(2,1)S(1)}, u32[]{:S(2)}, u32[]{:S(2)}) %collective-permute-start.7) | collective-permute-done | bytes 262176 | tf_op jit(solution)/shard_map/ppermute | solution.py:18
  157.3 14.2 %collective-permute-start.8 = (bf16[256,512]{1,0:T(8,128)(2,1)S(1)}, bf16[256,512]{1,0:T(8,128)(2,1)S(1)}, u32[]{:S(2)}, u32[]{:S(2)}) collective-permute-start(bf16[256,512]{1,0:T(8,128)(2,1)S(1)} %collective-permute-done.7), channel_id=1, source_target_pairs={{0,4},{4,8},{8,12},{1,5},{5,9},{9,13},{2,6},{6,10},{10,14},{3,7},{... | collective-permute-start | bytes 786440 | tf_op jit(solution)/shard_map/ppermute | solution.py:18
  171.5 1.6 fusion.7
  173.1 7.8 %collective-permute-done.8 = bf16[256,512]{1,0:T(8,128)(2,1)S(1)} collective-permute-done((bf16[256,512]{1,0:T(8,128)(2,1)S(1)}, bf16[256,512]{1,0:T(8,128)(2,1)S(1)}, u32[]{:S(2)}, u32[]{:S(2)}) %collective-permute-start.8) | collective-permute-done | bytes 262176 | tf_op jit(solution)/shard_map/ppermute | solution.py:18
  181.2 1.4 copy-done.12
  182.6 4.7 fusion.53
  187.3 6.0 %fusion.8 = bf16[256,4,256]{2,0,1:T(8,128)(2,1)S(1)} fusion(f32[4,256]{1,0:T(4,128)S(1)} %fusion.53, bf16[2304,512]{1,0:T(8,128)(2,1)} %copy-done.12, pred[256,2304]{0,1:T(8,128)(4,1)S(1)} %fusion.7, bf16[32,4,8,256]{3,2,1,0:T(8,128)(2,1)S(1)} %bitcast.79), kind=kOutput, calls=%fused_computation.17 | convolution fusion | flops 2427981056 | bytes 4001792 | tf_op jit(solution)/shard_map/htk,kd->thd/dot_general | solution.py:49
  193.3 6.1 %all-gather.4.cloned.1.call-done = bf16[1024,4096]{1,0:T(8,128)(2,1)} async-done(((bf16[1024,1024]{1,0:T(8,128)(2,1)}), bf16[1024,4096]{1,0:T(8,128)(2,1)}) %all-gather.4.cloned.1.call-update) | async-done | bytes 8388624 | tf_op jit(solution)/shard_map/all_gather | solution.py:94
  199.4 7.1 %convolution_convert_fusion = bf16[256,4096]{1,0:T(8,128)(2,1)} fusion(bf16[256,1024]{0,1:T(8,128)(2,1)S(1)} %bitcast.71, bf16[1024,4096]{1,0:T(8,128)(2,1)} %all-gather.4.cloned.1.call-done), kind=kOutput, calls=%fused_computation.6 | convolution fusion | flops 2148532224 | bytes 11010048 | tf_op jit(solution)/shard_map/dot_general | solution.py:92
  207.5 38.5 %reduce-scatter.2.cloned.1.call-done = bf16[64,4096]{1,0:T(8,128)(2,1)} async-done(((bf16[256,4096]{1,0:T(8,128)(2,1)}), bf16[64,4096]{1,0:T(8,128)(2,1)}) %reduce-scatter.2.cloned.1.call-update) | async-done | bytes 524304 | tf_op jit(solution)/shard_map/reduce_scatter | solution.py:97
  249.3 148.0 %all-gather.8.cloned.1.call-done = bf16[4096,1024]{1,0:T(8,128)(2,1)} async-done(((bf16[1024,1024]{1,0:T(8,128)(2,1)}), bf16[4096,1024]{1,0:T(8,128)(2,1)}) %all-gather.8.cloned.1.call-update) | async-done | bytes 8388624 | tf_op jit(solution)/shard_map/all_gather | solution.py:105
  397.3 22.9 %all-gather.6.cloned.1.call-done = bf16[256,4096]{1,0:T(8,128)(2,1)} async-done(((bf16[64,4096]{1,0:T(8,128)(2,1)}), bf16[256,4096]{1,0:T(8,128)(2,1)}) %all-gather.6.cloned.1.call-update) | async-done | bytes 2097168 | tf_op jit(solution)/shard_map/all_gather | solution.py:101
  420.2 6.3 %convolution_convert_fusion.1 = bf16[256,1024]{1,0:T(8,128)(2,1)S(1)} fusion(bf16[256,4096]{1,0:T(8,128)(2,1)} %all-gather.6.cloned.1.call-done, bf16[4096,1024]{1,0:T(8,128)(2,1)} %all-gather.8.cloned.1.call-done), kind=kOutput, calls=%fused_computation.18 | convolution fusion | flops 2147745792 | bytes 11010048 | tf_op jit(solution)/shard_map/dot_general | solution.py:103
  426.6 3.4 collective-permute-start.9
  435.4 2.8 convert_multiply_fusion.2
  438.3 1.4 slice.296
  439.7 1.5 slice.297
  441.2 1.5 slice.295
  442.6 1.5 slice.299
  444.1 2.5 multiply_add_fusion.1
  446.6 1.7 slice.302
  448.3 1.7 slice.303
  451.5 1.9 multiply_add_fusion.2
  454.8 1.6 slice.307
  456.4 1.6 slice.311
  458.0 1.8 multiply_add_fusion.3
  461.1 1.5 slice.313
  462.6 1.5 slice.317
  464.1 1.6 multiply_add_fusion.4
  465.7 1.4 slice.320
  467.2 1.4 slice.321
  468.6 1.4 slice.319
  470.0 1.5 slice.323
  471.5 1.4 multiply_add_fusion.5
  485.0 1.4 fusion.50
  491.9 1.5 slice.318
  493.3 1.4 slice.343
  497.5 1.5 slice.312
  505.4 1.7 slice.349
  509.1 1.5 slice.294
  510.7 1.5 slice.351
  520.3 2.7 pad.114
  523.3 2.3 fusion.24
  525.8 2.7 pad.130
  529.6 2.7 pad.129
  533.2 16.5 %while.10 = (s32[]{:T(128)}, f32[1024]{0:T(1024)S(1)}, f32[1024]{0:T(1024)S(1)}, f32[1024]{0:T(1024)S(1)}, s32[]{:T(128)}) while((s32[]{:T(128)}, f32[1024]{0:T(1024)S(1)}, f32[1024]{0:T(1024)S(1)}, f32[1024]{0:T(1024)S(1)}, s32[]{:T(128)}) %tuple.63), condition=%wide.region_6.7_spmd, body=%wide.region_5.6_spmd.sunk | while | flops 2050 | bytes 32869 | solution.py:150
  533.2 4.2 collective-permute-start
  538.7 4.2 collective-permute-start
  544.2 4.2 collective-permute-start
  549.7 2.8 add_convert_fusion
  (195 shorter events, 57.5 us)
Async XLA Ops:
  7.2 424.9 %copy-start = (bf16[4,256,256]{2,1,0:T(8,128)(2,1)S(1)}, bf16[4,256,256]{2,1,0:T(8,128)(2,1)}, u32[]{:S(2)}) copy-start(bf16[4,256,256]{2,1,0:T(8,128)(2,1)} %param.22) | copy-start | bytes 1572868
  7.2 119.4 %copy-start.13 = (s32[1024]{0:T(1024)S(1)}, s32[1024]{0:T(1024)}, u32[]{:S(2)}) copy-start(s32[1024]{0:T(1024)} %param.17) | copy-start | bytes 12292
  7.2 192.2 %all-gather.4.cloned.1.call-start = ((), (), s32[]{:S(2)}) async-start(), calls=%async_computation.1 | async-start | bytes 10485760 | tf_op jit(solution)/shard_map/all_gather | solution.py:94
  7.9 238.0 %reduce-scatter.2.cloned.1.call-start = ((), (), s32[]{:S(2)}) async-start(), calls=%async_computation.2 | async-start | bytes 2621440 | tf_op jit(solution)/shard_map/reduce_scatter | solution.py:97
  15.4 12.7 %collective-permute-start.1 = (bf16[256,512]{1,0:T(8,128)(2,1)S(1)}, bf16[256,512]{1,0:T(8,128)(2,1)S(1)}, u32[]{:S(2)}, u32[]{:S(2)}) collective-permute-start(bf16[256,512]{1,0:T(8,128)(2,1)S(1)} %all_gather.12), channel_id=1, source_target_pairs={{0,4},{4,8},{8,12},{1,5},{5,9},{9,13},{2,6},{6,10},{10,14},{3,7},{... | collective-permute-start | bytes 786440 | tf_op jit(solution)/shard_map/ppermute | solution.py:18
  28.0 19.6 %collective-permute-start.2 = (bf16[256,512]{1,0:T(8,128)(2,1)S(1)}, bf16[256,512]{1,0:T(8,128)(2,1)S(1)}, u32[]{:S(2)}, u32[]{:S(2)}) collective-permute-start(bf16[256,512]{1,0:T(8,128)(2,1)S(1)} %collective-permute-done.1), channel_id=1, source_target_pairs={{0,4},{4,8},{8,12},{1,5},{5,9},{9,13},{2,6},{6,10},{10,14},{3,7},{... | collective-permute-start | bytes 786440 | tf_op jit(solution)/shard_map/ppermute | solution.py:18
  47.7 23.2 %collective-permute-start.3 = (bf16[256,512]{1,0:T(8,128)(2,1)S(1)}, bf16[256,512]{1,0:T(8,128)(2,1)S(1)}, u32[]{:S(2)}, u32[]{:S(2)}) collective-permute-start(bf16[256,512]{1,0:T(8,128)(2,1)S(1)} %collective-permute-done.2), channel_id=1, source_target_pairs={{0,4},{4,8},{8,12},{1,5},{5,9},{9,13},{2,6},{6,10},{10,14},{3,7},{... | collective-permute-start | bytes 786440 | tf_op jit(solution)/shard_map/ppermute | solution.py:18
  70.9 22.0 %collective-permute-start.4 = (bf16[256,512]{1,0:T(8,128)(2,1)S(1)}, bf16[256,512]{1,0:T(8,128)(2,1)S(1)}, u32[]{:S(2)}, u32[]{:S(2)}) collective-permute-start(bf16[256,512]{1,0:T(8,128)(2,1)S(1)} %collective-permute-done.3), channel_id=1, source_target_pairs={{0,4},{4,8},{8,12},{1,5},{5,9},{9,13},{2,6},{6,10},{10,14},{3,7},{... | collective-permute-start | bytes 786440 | tf_op jit(solution)/shard_map/ppermute | solution.py:18
  92.9 19.9 %collective-permute-start.5 = (bf16[256,512]{1,0:T(8,128)(2,1)S(1)}, bf16[256,512]{1,0:T(8,128)(2,1)S(1)}, u32[]{:S(2)}, u32[]{:S(2)}) collective-permute-start(bf16[256,512]{1,0:T(8,128)(2,1)S(1)} %collective-permute-done.4), channel_id=1, source_target_pairs={{0,4},{4,8},{8,12},{1,5},{5,9},{9,13},{2,6},{6,10},{10,14},{3,7},{... | collective-permute-start | bytes 786440 | tf_op jit(solution)/shard_map/ppermute | solution.py:18
  112.8 23.2 %collective-permute-start.6 = (bf16[256,512]{1,0:T(8,128)(2,1)S(1)}, bf16[256,512]{1,0:T(8,128)(2,1)S(1)}, u32[]{:S(2)}, u32[]{:S(2)}) collective-permute-start(bf16[256,512]{1,0:T(8,128)(2,1)S(1)} %collective-permute-done.5), channel_id=1, source_target_pairs={{0,4},{4,8},{8,12},{1,5},{5,9},{9,13},{2,6},{6,10},{10,14},{3,7},{... | collective-permute-start | bytes 786440 | tf_op jit(solution)/shard_map/ppermute | solution.py:18
  136.0 21.3 %collective-permute-start.7 = (bf16[256,512]{1,0:T(8,128)(2,1)S(1)}, bf16[256,512]{1,0:T(8,128)(2,1)S(1)}, u32[]{:S(2)}, u32[]{:S(2)}) collective-permute-start(bf16[256,512]{1,0:T(8,128)(2,1)S(1)} %collective-permute-done.6), channel_id=1, source_target_pairs={{0,4},{4,8},{8,12},{1,5},{5,9},{9,13},{2,6},{6,10},{10,14},{3,7},{... | collective-permute-start | bytes 786440 | tf_op jit(solution)/shard_map/ppermute | solution.py:18
  157.3 23.6 %collective-permute-start.8 = (bf16[256,512]{1,0:T(8,128)(2,1)S(1)}, bf16[256,512]{1,0:T(8,128)(2,1)S(1)}, u32[]{:S(2)}, u32[]{:S(2)}) collective-permute-start(bf16[256,512]{1,0:T(8,128)(2,1)S(1)} %collective-permute-done.7), channel_id=1, source_target_pairs={{0,4},{4,8},{8,12},{1,5},{5,9},{9,13},{2,6},{6,10},{10,14},{3,7},{... | collective-permute-start | bytes 786440 | tf_op jit(solution)/shard_map/ppermute | solution.py:18
  181.2 1.4 copy-start.12
  182.6 4.7 copy-start.28
  206.5 39.5 %copy-start.4 = (bf16[64,4096]{1,0:T(8,128)(2,1)S(1)}, bf16[64,4096]{1,0:T(8,128)(2,1)}, u32[]{:S(2)}) copy-start(bf16[64,4096]{1,0:T(8,128)(2,1)} %param.18) | copy-start | bytes 1572868
  206.5 41.6 %copy-start.14 = (f32[4096]{0:T(1024)S(1)}, f32[4096]{0:T(1024)}, u32[]{:S(2)}) copy-start(f32[4096]{0:T(1024)} %param.27) | copy-start | bytes 49156
  206.5 42.6 %copy-start.25 = (s32[1024]{0:T(1024)S(1)}, s32[1024]{0:T(1024)}, u32[]{:S(2)}) copy-start(s32[1024]{0:T(1024)} %param.26) | copy-start | bytes 12292
  206.5 42.7 %copy-start.24 = (f32[4,1024]{1,0:T(4,128)S(1)}, f32[4,1024]{1,0:T(4,128)}, u32[]{:S(2)}) copy-start(f32[4,1024]{1,0:T(4,128)} %param.21) | copy-start | bytes 49156
  206.5 190.8 %all-gather.8.cloned.1.call-start = ((), (), s32[]{:S(2)}) async-start(), calls=%async_computation.4 | async-start | bytes 10485760 | tf_op jit(solution)/shard_map/all_gather | solution.py:105
  207.3 212.9 %all-gather.6.cloned.1.call-start = ((), (), s32[]{:S(2)}) async-start(), calls=%async_computation.3 | async-start | bytes 2621440 | tf_op jit(solution)/shard_map/all_gather | solution.py:101
  247.3 0.8 copy-start.2
  426.6 4.7 collective-permute-start.9
  432.1 1.7 copy-start.5
  433.7 1.7 copy-start.26
  433.7 1.7 copy-start.27
  509.1 7.2 %copy-start.11 = (f32[3,1024]{1,0:T(4,128)S(1)}, f32[3,1024]{1,0:T(4,128)}, u32[]{:S(2)}) copy-start(f32[3,1024]{1,0:T(4,128)} %slice.341) | copy-start | bytes 36868
  509.1 7.2 %copy-start.23 = (f32[1,1024]{1,0:T(1,128)S(1)}, f32[1,1024]{1,0:T(1,128)}, u32[]{:S(2)}) copy-start(f32[1,1024]{1,0:T(1,128)} %slice.407) | copy-start | bytes 12292
  509.1 7.3 %copy-start.22 = (f32[1,1024]{1,0:T(1,128)S(1)}, f32[1,1024]{1,0:T(1,128)}, u32[]{:S(2)}) copy-start(f32[1,1024]{1,0:T(1,128)} %slice.381) | copy-start | bytes 12292
  509.1 7.4 %copy-start.9 = (f32[7,1024]{1,0:T(8,128)S(1)}, f32[7,1024]{1,0:T(8,128)}, u32[]{:S(2)}) copy-start(f32[7,1024]{1,0:T(8,128)} %slice.318) | copy-start | bytes 86020
  509.1 7.4 %copy-start.10 = (f32[7,1024]{1,0:T(8,128)S(1)}, f32[7,1024]{1,0:T(8,128)}, u32[]{:S(2)}) copy-start(f32[7,1024]{1,0:T(8,128)} %slice.343) | copy-start | bytes 86020
  509.1 8.9 %copy-start.7 = (f32[15,1024]{1,0:T(8,128)S(1)}, f32[15,1024]{1,0:T(8,128)}, u32[]{:S(2)}) copy-start(f32[15,1024]{1,0:T(8,128)} %slice.312) | copy-start | bytes 184324
  509.1 8.9 %copy-start.8 = (f32[15,1024]{1,0:T(8,128)S(1)}, f32[15,1024]{1,0:T(8,128)}, u32[]{:S(2)}) copy-start(f32[15,1024]{1,0:T(8,128)} %slice.345) | copy-start | bytes 184324
  512.2 6.8 %copy-start.6 = (f32[31,1024]{1,0:T(8,128)S(1)}, f32[31,1024]{1,0:T(8,128)}, u32[]{:S(2)}) copy-start(f32[31,1024]{1,0:T(8,128)} %slice.347) | copy-start | bytes 380932
  512.8 5.3 copy-start.21
  516.5 2.6 copy-start.20
  518.1 1.2 copy-start.19
  519.0 1.0 copy-start.3
  519.2 0.9 copy-start.18
  520.1 2.9 copy-start.17
  523.3 2.3 copy-start.16
  525.6 3.0 copy-start.15
  525.8 6.6 %copy-start.1 = (f32[256,1024]{1,0:T(8,128)S(1)}, f32[256,1024]{1,0:T(8,128)}, u32[]{:S(2)}) copy-start(f32[256,1024]{1,0:T(8,128)} %pad.114) | copy-start | bytes 3145732
  533.2 5.5 collective-permute-start
  538.7 5.5 collective-permute-start
  544.2 5.5 collective-permute-start
Sparse Core Ops, SparseCore 0:
  9.6 189.7 all-gather.3
  206.6 39.3 reduce-scatter.1
  247.6 149.6 all-gather.7
  399.4 20.7 all-gather.5
where the time goes:
time: 562 us; the launch traced here: 559 us
  waiting for transfers between devices  300 us (53%)
  starting transfers between devices  102 us (18%)
  local copies, waits for them, and re-layouts  77.2 us (14%)
  other arithmetic  32.9 us (6%)
  matrix products  24.8 us (4%)
  between operations  14.7 us (3%)
  blocking collectives  7.41 us (1%)
    all_gather x1, waiting for transfers between devices, local(): lax.all_gather(lru_weight, 'ctx', axis=0, tiled=True)  148 us
    ppermute x12, starting transfers between devices, shifted_2(): lax.ppermute(value, axis, [(source, source + steps) for source in range(i...  102 us
    ppermute x12, waiting for transfers between devices, shifted_2(): lax.ppermute(value, axis, [(source, source + steps) for source in range(i...  82.7 us
    slice x52, local copies, waits for them, and re-layouts, local(): lax.associative_scan(chain_link, (keep_factor, driven), axis=0)  61 us
    reduce_scatter x1, waiting for transfers between devices, local(): lax.psum_scatter(head_part.astype(jnp.bfloat16), 'mp', scatter_dimension=...  38.5 us
    all_gather x1, waiting for transfers between devices, local(): lax.all_gather(rms_scaled(resid_out, norm_gain), 'mp', axis=0, tiled=True)  22.9 us
    add x13, other arithmetic, chain_link(): return (former[0] * latter[0], latter[0] * former[1] + latter[1])  13.8 us
  transfers between devices with their start and end apart: 16, of which 16 were waited for; matrix products, arithmetic and copies ran while one was open for 3% of the time, Pallas kernels for 0%

commit v1 on v0

--- a/solution.py
+++ b/solution.py
@@ -3,6 +3,8 @@
 import jax
 import jax.numpy as jnp
 from jax import lax
+from jax.experimental import pallas as pl
+from jax.experimental.pallas import tpu as pltpu
 from jax.sharding import PartitionSpec as P
 
 HD = 256
@@ -99,57 +101,155 @@
     ).astype(jnp.float32)
     resid_out = (summed + residual.astype(jnp.float32)).astype(jnp.bfloat16)
     normed = lax.all_gather(rms_scaled(resid_out, norm_gain), "mp", axis=0, tiled=True)
-    channels = lru_weight.shape[1]
     lru_in = jnp.dot(
         normed,
         lax.all_gather(lru_weight, "ctx", axis=0, tiled=True),
         preferred_element_type=jnp.float32,
     ).astype(jnp.bfloat16)
-    rim_rows = shifted_2(lru_in[rows_here - (CONV - 1) :], "ctx", 1)
+    return resid_out, recurrence(
+        lru_in, segment_ids, conv_weight, gate_decay_w, gate_input_w,
+        gate_decay_b, gate_input_b, decay_codes,
+    )
+
+
+HALO = 16
+
+
+def scan_kernel(ext_ref, flags_ref, conv_ref, wd_ref, wi_ref, vec_ref, keep_ref, state_ref):
+    rows = state_ref.shape[0]
+    groups = rows // 8
+    flags = flags_ref[...]
+    row_in_group = lax.broadcasted_iota(jnp.int32, (groups, 8, BW), 1)
+    for block in range(state_ref.shape[1] // BW):
+        cols = slice(block * BW, (block + 1) * BW)
+        ext = ext_ref[:, cols].astype(jnp.float32)
+        acc = conv_ref[0:1, cols] * ext[HALO:]
+        for lag in range(1, CONV):
+            moved = pltpu.roll(ext, lag, 0)[HALO:]
+            acc = acc + jnp.where(flags[:, lag : lag + 1] > 0.5, conv_ref[lag : lag + 1, cols] * moved, 0.0)
+        conv_out = acc.astype(jnp.bfloat16)
+        decay_gate = jax.nn.sigmoid(
+            jnp.dot(conv_out, wd_ref[block], preferred_element_type=jnp.float32) + vec_ref[0:1, cols]
+        )
+        input_gate = jax.nn.sigmoid(
+            jnp.dot(conv_out, wi_ref[block], preferred_element_type=jnp.float32) + vec_ref[1:2, cols]
+        )
+        log_decay = -8.0 * decay_gate * vec_ref[2:3, cols]
+        restart = flags[:, 0:1] > 0.5
+        keep = jnp.where(restart, 0.0, jnp.exp(log_decay))
+        x = 2.0 * log_decay
+        poly = 1.0 + x * (1.0 / 6.0)
+        for order in (5.0, 4.0, 3.0, 2.0):
+            poly = 1.0 + x * (1.0 / order) * poly
+        scale = jnp.where(restart, 1.0, jnp.sqrt(-x * poly))
+        state = scale * input_gate * conv_out.astype(jnp.float32)
+        keep = keep.reshape(groups, 8, BW)
+        state = state.reshape(groups, 8, BW)
+        for shift in (1, 2, 4):
+            inside = row_in_group >= shift
+            before_state = jnp.where(inside, pltpu.roll(state, shift, 1), 0.0)
+            before_keep = jnp.where(inside, pltpu.roll(keep, shift, 1), 1.0)
+            state = state + keep * before_state
+            keep = keep * before_keep
+        keep_carry = jnp.ones((1, BW), jnp.float32)
+        state_carry = jnp.zeros((1, BW), jnp.float32)
+        for group in range(groups):
+            rows_now = slice(group * 8, group * 8 + 8)
+            state_now = state[group] + keep[group] * state_carry
+            keep_now = keep[group] * keep_carry
+            state_ref[rows_now, cols] = state_now
+            keep_ref[rows_now, cols] = keep_now
+            state_carry = state_now[7:8]
+            keep_carry = keep_now[7:8]
+
+
+def recurrence(
+    lru_in, segment_ids, conv_weight, gate_decay_w, gate_input_w, gate_decay_b, gate_input_b, decay_codes
+):
+    rows_here, channels = lru_in.shape
+    ctx_index = lax.axis_index("ctx")
+    rim_rows = shifted_2(lru_in[rows_here - HALO :], "ctx", 1)
     extended = jnp.concatenate([rim_rows, lru_in], axis=0)
-    ext_seg = lax.dynamic_slice_in_dim(
-        pad_seg, ctx_index * rows_here + WIN - (CONV - 1), rows_here + CONV - 1
-    )
-    conv_acc = jnp.zeros((rows_here, channels), jnp.float32)
-    for offset in range(CONV):
-        lag_rows = CONV - 1 - offset
-        shifted = extended[lag_rows : lag_rows + rows_here].astype(jnp.float32)
-        same_doc = (ext_seg[lag_rows : lag_rows + rows_here] == query_seg)[:, None]
-        conv_acc = conv_acc + jnp.where(same_doc, conv_weight[offset] * shifted, 0.0)
-    conv_out = conv_acc.astype(jnp.bfloat16)
-    blocks_here = channels // BW
-    grouped = conv_out.reshape(rows_here, blocks_here, BW)
-    decay_gate = jax.nn.sigmoid(
-        jnp.einsum(
-            "tbi,bij->tbj", grouped, gate_decay_w, preferred_element_type=jnp.float32
-        ).reshape(rows_here, channels)
-        + gate_decay_b
-    )
-    input_gate = jax.nn.sigmoid(
-        jnp.einsum(
-            "tbi,bij->tbj", grouped, gate_input_w, preferred_element_type=jnp.float32
-        ).reshape(rows_here, channels)
-        + gate_input_b
-    )
+    pad_seg = jnp.concatenate([jnp.full((CONV - 1,), -1, jnp.int32), segment_ids])
+    ext_seg = lax.dynamic_slice_in_dim(pad_seg, ctx_index * rows_here, rows_here + CONV - 1)
+    query_seg = ext_seg[CONV - 1 :]
+    lagged = [ext_seg[CONV - 1 - lag : CONV - 1 - lag + rows_here] == query_seg for lag in range(CONV)]
+    flags = jnp.stack([~lagged[1]] + lagged[1:], axis=1).astype(jnp.float32)
     levels = jnp.arange(LEVELS, dtype=jnp.int32)
     decay_rate = jnp.sum(
         jnp.where(decay_codes[:, None] == levels[None, :], decay_rates()[None, :], 0.0), axis=1
     )
-    log_decay = -8.0 * decay_gate * decay_rate
-    restart = (query_seg != ext_seg[CONV - 2 : CONV - 2 + rows_here])[:, None]
-    keep_factor = jnp.where(restart, 0.0, jnp.exp(log_decay))
-    input_scale = jnp.where(restart, 1.0, jnp.sqrt(-jnp.expm1(2.0 * log_decay)))
-    driven = input_scale * input_gate * conv_out.astype(jnp.float32)
-    cum_keep, local_state = lax.associative_scan(chain_link, (keep_factor, driven), axis=0)
-    block_keep = cum_keep[rows_here - 1]
-    block_state = local_state[rows_here - 1]
-
-    def relay_turn(turn_index, state_in):
-        return shifted_2(block_keep * state_in + block_state, "ctx", 1)
-
-    incoming = lax.fori_loop(0, lax.axis_size("ctx") - 1, relay_turn, jnp.zeros_like(block_state))
+    vectors = jnp.stack([gate_decay_b, gate_input_b, decay_rate])
+    full = jax.ShapeDtypeStruct((rows_here, channels), jnp.float32)
+    cum_keep, local_state = pl.pallas_call(
+        scan_kernel,
+        out_shape=(full, full),
+        compiler_params=pltpu.CompilerParams(vmem_limit_bytes=40 * 1024 * 1024),
+    )(extended, flags, conv_weight, gate_decay_w, gate_input_w, vectors)
+    ends = jnp.stack([cum_keep[rows_here - 1], local_state[rows_here - 1]])
+    all_ends = lax.all_gather(ends, "ctx", axis=0)
+    incoming = jnp.zeros((channels,), jnp.float32)
+    for source in range(lax.axis_size("ctx") - 1):
+        incoming = jnp.where(
+            source < ctx_index, all_ends[source, 0] * incoming + all_ends[source, 1], incoming
+        )
     states = local_state + cum_keep * incoming[None, :]
-    return (resid_out, states.astype(jnp.bfloat16))
+    return states.astype(jnp.bfloat16)
+
+
+def local_stationary(
+    queries,
+    keyvals,
+    segment_ids,
+    residual,
+    out_weight,
+    lru_weight,
+    conv_weight,
+    gate_decay_w,
+    gate_input_w,
+    gate_decay_b,
+    gate_input_b,
+    decay_codes,
+    norm_gain,
+):
+    rows_here = queries.shape[0]
+    tokens = segment_ids.shape[0]
+    ctx_index = lax.axis_index("ctx")
+    blocks, members = lax.axis_size("ctx"), lax.axis_size("mp")
+    piece = rows_here // members
+    cols = out_weight.shape[1]
+    keys_all = lax.all_gather(keyvals, ("ctx", "mp"), axis=0, tiled=True)
+    residual_cols = lax.all_to_all(residual, "ctx", split_axis=1, concat_axis=0, tiled=True)
+    query_seg = lax.dynamic_slice_in_dim(segment_ids, ctx_index * rows_here, rows_here)
+    query_pos = ctx_index * rows_here + jnp.arange(rows_here, dtype=jnp.int32)
+    distance = query_pos[:, None] - jnp.arange(tokens, dtype=jnp.int32)[None, :]
+    allowed = (distance >= 0) & (distance < WIN) & (query_seg[:, None] == segment_ids[None, :])
+    attended = attend_local(queries, keys_all, allowed)
+    attended_all = lax.all_gather(attended, "ctx", axis=0, tiled=True)
+    head_part = jnp.dot(attended_all, out_weight, preferred_element_type=jnp.float32)
+    summed = lax.psum_scatter(
+        head_part.astype(jnp.bfloat16).reshape(blocks, rows_here, cols), "mp", scatter_dimension=1, tiled=True
+    )
+    resid_cols = (
+        summed.reshape(blocks * piece, cols).astype(jnp.float32) + residual_cols.astype(jnp.float32)
+    ).astype(jnp.bfloat16)
+    resid_out = lax.all_to_all(resid_cols, "ctx", split_axis=0, concat_axis=1, tiled=True)
+    resid_f32 = resid_cols.astype(jnp.float32)
+    squares = jnp.sum(resid_f32 * resid_f32, axis=-1).reshape(blocks, piece)
+    all_squares = lax.all_gather(squares, ("ctx", "mp"), axis=0).reshape(blocks, members, blocks, piece)
+    own_squares = lax.dynamic_index_in_dim(all_squares, ctx_index, 2, keepdims=False)
+    mean_square = jnp.sum(own_squares, axis=0).reshape(rows_here) / residual.shape[1]
+    inverse = lax.rsqrt(mean_square + 1e-06)
+    gain = lax.dynamic_slice_in_dim(norm_gain, ctx_index * cols, cols)
+    gained = (resid_f32 * gain).astype(jnp.bfloat16).reshape(blocks, piece, cols)
+    gained_all = lax.all_gather(gained, "mp", axis=1, tiled=True).reshape(tokens, cols)
+    partial = jnp.dot(gained_all, lru_weight, preferred_element_type=jnp.float32).astype(jnp.bfloat16)
+    mixed = lax.psum_scatter(partial, "ctx", scatter_dimension=0, tiled=True)
+    lru_in = (mixed.astype(jnp.float32) * inverse[:, None]).astype(jnp.bfloat16)
+    return resid_out, recurrence(
+        lru_in, segment_ids, conv_weight, gate_decay_w, gate_input_w,
+        gate_decay_b, gate_input_b, decay_codes,
+    )
 
 
 def solution(mesh):
@@ -169,4 +269,10 @@
         P(),
     )
     out_specs = (P(("groups", "ctx", "mp"), None), P(("groups", "ctx"), "mp"))
-    return jax.shard_map(local, mesh=mesh, in_specs=in_specs, out_specs=out_specs, check_vma=False)
+
+    def body(*args):
+        segment_ids, out_weight = args[2], args[4]
+        stationary = segment_ids.shape[0] <= lax.axis_size("ctx") * out_weight.shape[1] // 2
+        return (local_stationary if stationary else local)(*args)
+
+    return jax.shard_map(body, mesh=mesh, in_specs=in_specs, out_specs=out_specs, check_vma=False)

time: 562 us -> 256 us (0.46)
  waiting for transfers between devices: 300 us -> 146 us
  starting transfers between devices: 102 us -> 13.7 us
  local copies, waits for them, and re-layouts: 77.2 us -> 7.81 us
  blocking collectives: 7.41 us -> 46.8 us
  other arithmetic: 32.9 us -> 8.9 us
  matrix products: 24.8 us -> 14.7 us
    ppermute x12 -> x1, starting transfers between devices: 102 us -> 5.28 us  [shifted_2(): lax.ppermute(value, axis, [(source, source + steps) for source in range(i...]
    ppermute x12 -> x1, waiting for transfers between devices: 82.7 us -> 0.01 us  [shifted_2(): lax.ppermute(value, axis, [(source, source + steps) for source in range(i...]
    all_gather x3, waiting for transfers between devices: 177 us -> 109 us  [the longest x1 45.3 us: local_stationary(): attended_all = lax.all_gather(attended, 'ctx', axis=0, tiled=True)]
    slice x54 -> x3, local copies, waits for them, and re-layouts: 61 us -> 0.02 us  [the longest x2 0.01 us: recurrence(): ends = jnp.stack([cum_keep[rows_here - 1], local_state[rows_here - 1]])]
    all_gather x1 -> x2, blocking collectives: 7.41 us -> 46.8 us  [the longest x1 33.7 us: local_stationary(): lax.all_gather(squares, ('ctx', 'mp'), axis=0)]
    add x33 -> x1, other arithmetic: 16.1 us -> 0.01 us  [local_stationary(): query_pos = ctx_index * rows_here + jnp.arange(rows_here, dtype=jnp.int32)]
    reduce_scatter x1 -> x2, waiting for transfers between devices: 38.5 us -> 23.3 us  [the longest x1 12.8 us: local_stationary(): mixed = lax.psum_scatter(partial, 'ctx', scatter_dimension=0, tiled=True)]
    all_to_all x0 -> x2, waiting for transfers between devices: none -> 13.3 us  [the longest x1 13.3 us: local_stationary(): lax.all_to_all(residual, 'ctx', split_axis=1, concat_axis=0, tiled=True)]
  transfers between devices with their start and end apart: 16 -> 8, of which waited for: 16 -> 6; matrix products, arithmetic and copies ran while one was open for 3% -> 3% of each run, Pallas kernels for 0% -> 0%
where the time goes in v1:
time: 256 us; the launch traced here: 255 us
  waiting for transfers between devices  146 us (57%)
  blocking collectives  46.8 us (18%)
  matrix products  14.7 us (6%)
  between operations  14 us (5%)
  starting transfers between devices  13.7 us (5%)
  other arithmetic  8.9 us (3%)
  local copies, waits for them, and re-layouts  7.81 us (3%)
  Pallas kernels  3.09 us (1%)
    all_gather x1, waiting for transfers between devices, local_stationary(): attended_all = lax.all_gather(attended, 'ctx', axis=0, tiled=True)  45.3 us
    all_gather x1, waiting for transfers between devices, local_stationary(): keys_all = lax.all_gather(keyvals, ('ctx', 'mp'), axis=0, tiled=True)  41 us
    all_gather x1, blocking collectives, local_stationary(): lax.all_gather(squares, ('ctx', 'mp'), axis=0)  33.7 us
    all_gather x1, waiting for transfers between devices, local_stationary(): lax.all_gather(gained, 'mp', axis=1, tiled=True).reshape(tokens, cols)  22.7 us
    all_to_all x1, waiting for transfers between devices, local_stationary(): lax.all_to_all(residual, 'ctx', split_axis=1, concat_axis=0, tiled=True)  13.3 us
    all_gather x1, blocking collectives, recurrence(): all_ends = lax.all_gather(ends, 'ctx', axis=0)  13.1 us
    reduce_scatter x1, waiting for transfers between devices, local_stationary(): mixed = lax.psum_scatter(partial, 'ctx', scatter_dimension=0, tiled=True)  12.8 us
    reduce_scatter x1, waiting for transfers between devices, local_stationary(): lax.psum_scatter(head_part.astype(jnp.bfloat16).reshape(blocks, rows_here...  10.4 us
  transfers between devices with their start and end apart: 8, of which 6 were waited for; matrix products, arithmetic and copies ran while one was open for 3% of the time, Pallas kernels for 0%

profile of v1, /device:TPU:0, one launch (start us, length us, event | category | flops | bytes accessed | tf_op | source)
XLA Modules:
  0.0 255.4 jit_solution(17515531368981980832)
XLA Ops:
  7.2 0.0 copy-start
  7.2 0.0 all-gather.8.cloned.1.call-start
  7.2 0.7 all-gather.8.cloned.1.call-update
  7.9 0.0 all-gather.10.cloned.1.call-start
  8.0 0.8 dynamic_slice.13
  8.7 1.1 fusion.13
  9.8 41.0 %all-gather.8.cloned.1.call-done = bf16[1024,512]{1,0:T(8,128)(2,1)} async-done(((bf16[64,512]{1,0:T(8,128)(2,1)}), bf16[1024,512]{1,0:T(8,128)(2,1)}) %all-gather.8.cloned.1.call-update) | async-done | bytes 1048592 | tf_op jit(solution)/shard_map/all_gather | solution.py:221
  50.8 1.9 fusion.14
  52.8 0.0 copy-start.7
  52.8 2.1 fusion.22
  54.9 0.0 copy-done.7
  54.9 1.6 fusion.6
  56.5 0.0 all-gather.10.cloned.1.call-update
  56.5 0.0 reduce-scatter.3.cloned.1.call-start
  56.5 45.3 %all-gather.10.cloned.1.call-done = bf16[1024,1024]{0,1:T(8,128)(2,1)} async-done(((bf16[256,1024]{0,1:T(8,128)(2,1)}), bf16[1024,1024]{0,1:T(8,128)(2,1)}) %all-gather.10.cloned.1.call-update) | async-done | bytes 2097168 | tf_op jit(solution)/shard_map/all_gather | solution.py:228
  101.8 0.0 copy-done
  101.8 5.3 %convolution_convert_fusion.1 = bf16[1024,1024]{1,0:T(8,128)(2,1)} fusion(bf16[1024,1024]{0,1:T(8,128)(2,1)} %all-gather.10.cloned.1.call-done, bf16[1024,1024]{1,0:T(8,128)(2,1)S(1)} %copy-done), kind=kOutput, calls=%fused_computation.10 | convolution fusion | flops 2148532224 | bytes 6291456 | tf_op jit(solution)/shard_map/dot_general | solution.py:229
  107.1 0.0 copy-start.6
  107.1 0.0 reduce-scatter.3.cloned.1.call-update
  107.1 1.0 copy-done.6
  108.1 0.8 copy.58
  109.0 3.5 %all-to-all-start = ((bf16[64,4,1024]{2,0,1:T(8,128)(2,1)}), bf16[64,4,1024]{2,0,1:T(8,128)(2,1)S(1)}, u32[]{:S(2)}, u32[]{:S(2)}) async-start(bf16[64,4,1024]{2,0,1:T(8,128)(2,1)} %bitcast.53), calls=%async_computation.1 | async-start | bytes 1048576 | tf_op jit(solution)/shard_map/all_to_all | solution.py:222
  112.5 0.0 all-gather.12.cloned.1.call-start
  112.5 0.7 dynamic_slice.14
  113.2 13.3 %all-to-all-done = bf16[64,4,1024]{2,0,1:T(8,128)(2,1)S(1)} async-done(((bf16[64,4,1024]{2,0,1:T(8,128)(2,1)}), bf16[64,4,1024]{2,0,1:T(8,128)(2,1)S(1)}, u32[]{:S(2)}, u32[]{:S(2)}) %all-to-all-start) | async-done | bytes 524320 | tf_op jit(solution)/shard_map/all_to_all | solution.py:222
  126.5 10.4 %reduce-scatter.3.cloned.1.call-done = bf16[4,64,1024]{2,1,0:T(8,128)(2,1)} async-done(((bf16[4,256,1024]{2,1,0:T(8,128)(2,1)}), bf16[4,64,1024]{2,1,0:T(8,128)(2,1)}) %reduce-scatter.3.cloned.1.call-update) | async-done | bytes 524304 | tf_op jit(solution)/shard_map/reduce_scatter | solution.py:230
  136.9 1.3 fusion.8
  138.3 0.0 copy-start.4
  138.3 0.8 copy-done.4
  139.0 0.9 fusion.7
  140.0 0.0 all-gather.12.cloned.1.call-update
  140.0 0.0 reduce-scatter.5.cloned.1.call-start
  140.0 22.7 %all-gather.12.cloned.1.call-done = bf16[4,256,1024]{2,1,0:T(8,128)(2,1)} async-done(((bf16[4,64,1024]{2,1,0:T(8,128)(2,1)}), bf16[4,256,1024]{2,1,0:T(8,128)(2,1)}) %all-gather.12.cloned.1.call-update) | async-done | bytes 2097168 | tf_op jit(solution)/shard_map/all_gather | solution.py:245
  162.7 5.9 %convolution_convert_fusion = bf16[1024,1024]{1,0:T(8,128)(2,1)} fusion(bf16[1024,1024]{1,0:T(8,128)(2,1)} %bitcast.69, bf16[1024,1024]{1,0:T(8,128)(2,1)} %param.18), kind=kOutput, calls=%fused_computation.9 | convolution fusion | flops 2148532224 | bytes 6291456 | tf_op jit(solution)/shard_map/dot_general | solution.py:246
  168.6 0.0 reduce-scatter.5.cloned.1.call-update
  168.7 0.6 copy-done.8
  169.3 0.1 pad_dynamic-slice_fusion
  169.4 0.1 fusion.19
  169.5 0.0 copy-start.1
  169.5 0.0 copy-start.2
  169.5 0.0 copy-start.3
  169.6 4.7 %all-to-all-start.1 = ((bf16[4,64,1024]{2,1,0:T(8,128)(2,1)}), bf16[4,64,1024]{2,1,0:T(8,128)(2,1)}, u32[]{:S(2)}, u32[]{:S(2)}) async-start(bf16[4,64,1024]{2,1,0:T(8,128)(2,1)} %copy-done.4), calls=%async_computation.2 | async-start | bytes 1048576 | tf_op jit(solution)/shard_map/all_to_all | solution.py:236
  174.3 0.0 copy-done.11
  174.3 0.1 select_reduce_fusion
  174.4 0.0 copy-done.9
  174.4 0.0 copy-done.10
  174.4 33.7 %all-gather.2 = f32[16,4,64]{2,1,0:T(4,128)S(1)} all-gather(f32[1,4,64]{2,1,0:T(4,128)S(1)} %bitcast.66), channel_id=2, replica_groups=mesh['groups'=2,'ctx'=4,'mp'=4] {'ctx','mp'}, dimensions={0}, use_global_device_ids=true | all-gather | bytes 17408 | tf_op jit(solution)/shard_map/all_gather | solution.py:239
  208.1 0.1 rsqrt.11
  208.2 12.8 %reduce-scatter.5.cloned.1.call-done = bf16[256,1024]{1,0:T(8,128)(2,1)} async-done(((bf16[1024,1024]{1,0:T(8,128)(2,1)}), bf16[256,1024]{1,0:T(8,128)(2,1)}) %reduce-scatter.5.cloned.1.call-update) | async-done | bytes 524304 | tf_op jit(solution)/shard_map/reduce_scatter | solution.py:247
  221.1 1.2 multiply_convert_fusion
  222.3 0.0 copy-start.5
  222.3 0.8 copy-done.5
  223.1 5.3 %collective-permute-start = (bf16[16,1024]{1,0:T(8,128)(2,1)S(1)}, bf16[16,1024]{1,0:T(8,128)(2,1)S(1)}, u32[]{:S(2)}, u32[]{:S(2)}) collective-permute-start(bf16[16,1024]{1,0:T(8,128)(2,1)S(1)} %slice.62), channel_id=1, source_target_pairs={{0,4},{4,8},{8,12},{1,5},{5,9},{9,13},{2,6},{6,10},{10,14},{3,7},{... | collective-permute-start | bytes 98312 | tf_op jit(solution)/shard_map/ppermute | solution.py:20
  228.4 0.1 copy.46.flags_ref
  228.5 0.0 all-to-all-done.1
  228.5 1.9 copy.52
  230.4 0.0 collective-permute-done
  230.4 1.1 pad_maximum_fusion.ext_ref
  231.5 0.0 copy-done.1
  231.5 0.0 copy-done.2
  231.5 0.0 copy-done.3
  231.5 3.1 %shard_map.140 = (f32[256,1024]{1,0:T(8,128)S(1)}, f32[256,1024]{1,0:T(8,128)S(1)}) custom-call(bf16[272,1024]{1,0:T(8,128)(2,1)S(1)} %pad_maximum_fusion.ext_ref, f32[256,4]{1,0:T(8,128)S(1)} %copy.46.flags_ref, f32[4,1024]{1,0:T(4,128)S(1)} %copy-done.3, bf16[4,256,256]{2,1,0:T(8,128)(2,1)S(1)} %copy-done.1, bf16[4,256,256]{2,1,0:T(8,128)(2,1)S(1)} %copy-done.2, ...), custom_call_target="tpu_custom_call" | custom-call | tf_op jit(solution)/shard_map/pallas_call | solution.py:184
  234.7 13.1 %all-gather.3 = f32[4,2,1024]{2,1,0:T(2,128)S(1)} all-gather(f32[1,2,1024]{2,1,0:T(2,128)S(1)} %maximum_bitcast_fusion), channel_id=3, replica_groups=mesh['groups'=2,'ctx'=4,'mp'=4] {'ctx'}, dimensions={0}, use_global_device_ids=true | all-gather | bytes 40960 | tf_op jit(solution)/shard_map/all_gather | solution.py:190
  247.8 1.0 add_convert_fusion
  (20 shorter events, 0.2 us)
Async XLA Ops:
  7.2 94.6 %copy-start = (bf16[1024,1024]{1,0:T(8,128)(2,1)S(1)}, bf16[1024,1024]{1,0:T(8,128)(2,1)}, u32[]{:S(2)}) copy-start(bf16[1024,1024]{1,0:T(8,128)(2,1)} %param.17) | copy-start | bytes 6291460
  7.2 43.7 %all-gather.8.cloned.1.call-start = ((), (), s32[]{:S(2)}) async-start(), calls=%async_computation.4 | async-start | bytes 1114112 | tf_op jit(solution)/shard_map/all_gather | solution.py:221
  7.9 93.9 %all-gather.10.cloned.1.call-start = ((), (), s32[]{:S(2)}) async-start(), calls=%async_computation.5 | async-start | bytes 2621440 | tf_op jit(solution)/shard_map/all_gather | solution.py:228
  52.8 2.1 copy-start.7
  56.5 80.5 %reduce-scatter.3.cloned.1.call-start = ((), (), s32[]{:S(2)}) async-start(), calls=%async_computation.6 | async-start | bytes 2621440 | tf_op jit(solution)/shard_map/reduce_scatter | solution.py:230
  107.1 1.0 copy-start.6
  109.0 17.5 %all-to-all-start = ((bf16[64,4,1024]{2,0,1:T(8,128)(2,1)}), bf16[64,4,1024]{2,0,1:T(8,128)(2,1)S(1)}, u32[]{:S(2)}, u32[]{:S(2)}) async-start(bf16[64,4,1024]{2,0,1:T(8,128)(2,1)} %bitcast.53), calls=%async_computation.1 | async-start | bytes 1048576 | tf_op jit(solution)/shard_map/all_to_all | solution.py:222
  112.5 50.3 %all-gather.12.cloned.1.call-start = ((), (), s32[]{:S(2)}) async-start(), calls=%async_computation.7 | async-start | bytes 2621440 | tf_op jit(solution)/shard_map/all_gather | solution.py:245
  138.3 0.8 copy-start.4
  140.0 81.1 %reduce-scatter.5.cloned.1.call-start = ((), (), s32[]{:S(2)}) async-start(), calls=%async_computation.8 | async-start | bytes 2621440 | tf_op jit(solution)/shard_map/reduce_scatter | solution.py:247
  168.6 0.7 copy-start.8
  168.6 5.7 %copy-start.11 = (s32[1024]{0:T(1024)S(1)}, s32[1024]{0:T(1024)}, u32[]{:S(2)}) copy-start(s32[1024]{0:T(1024)} %param.24) | copy-start | bytes 12292
  168.6 5.8 %copy-start.9 = (f32[1024]{0:T(1024)S(1)}, f32[1024]{0:T(1024)}, u32[]{:S(2)}) copy-start(f32[1024]{0:T(1024)} %param.23) | copy-start | bytes 12292
  168.6 5.8 %copy-start.10 = (f32[1024]{0:T(1024)S(1)}, f32[1024]{0:T(1024)}, u32[]{:S(2)}) copy-start(f32[1024]{0:T(1024)} %param.22) | copy-start | bytes 12292
  169.5 62.0 %copy-start.1 = (bf16[4,256,256]{2,1,0:T(8,128)(2,1)S(1)}, bf16[4,256,256]{2,1,0:T(8,128)(2,1)}, u32[]{:S(2)}) copy-start(bf16[4,256,256]{2,1,0:T(8,128)(2,1)} %wd_ref.1) | copy-start | bytes 1572868
  169.5 62.0 %copy-start.2 = (bf16[4,256,256]{2,1,0:T(8,128)(2,1)S(1)}, bf16[4,256,256]{2,1,0:T(8,128)(2,1)}, u32[]{:S(2)}) copy-start(bf16[4,256,256]{2,1,0:T(8,128)(2,1)} %wi_ref.1) | copy-start | bytes 1572868
  169.5 62.0 %copy-start.3 = (f32[4,1024]{1,0:T(4,128)S(1)}, f32[4,1024]{1,0:T(4,128)}, u32[]{:S(2)}) copy-start(f32[4,1024]{1,0:T(4,128)} %conv_ref.1) | copy-start | bytes 49156
  169.6 59.0 %all-to-all-start.1 = ((bf16[4,64,1024]{2,1,0:T(8,128)(2,1)}), bf16[4,64,1024]{2,1,0:T(8,128)(2,1)}, u32[]{:S(2)}, u32[]{:S(2)}) async-start(bf16[4,64,1024]{2,1,0:T(8,128)(2,1)} %copy-done.4), calls=%async_computation.2 | async-start | bytes 1048576 | tf_op jit(solution)/shard_map/all_to_all | solution.py:236
  222.3 0.8 copy-start.5
  223.1 7.4 %collective-permute-start = (bf16[16,1024]{1,0:T(8,128)(2,1)S(1)}, bf16[16,1024]{1,0:T(8,128)(2,1)S(1)}, u32[]{:S(2)}, u32[]{:S(2)}) collective-permute-start(bf16[16,1024]{1,0:T(8,128)(2,1)S(1)} %slice.62), channel_id=1, source_target_pairs={{0,4},{4,8},{8,12},{1,5},{5,9},{9,13},{2,6},{6,10},{10,14},{3,7},{... | collective-permute-start | bytes 98312 | tf_op jit(solution)/shard_map/ppermute | solution.py:20
Sparse Core Ops, SparseCore 0:
  10.2 40.6 all-gather.7
  56.6 45.1 all-gather.9
  107.3 29.6 reduce-scatter.2
  140.1 22.5 all-gather.11
  168.8 52.2 reduce-scatter.4

commit v2 on v1

--- a/solution.py
+++ b/solution.py
@@ -1,3 +1,4 @@
+import functools
 import math
 
 import jax
@@ -163,13 +164,8 @@
             keep_carry = keep_now[7:8]
 
 
-def recurrence(
-    lru_in, segment_ids, conv_weight, gate_decay_w, gate_input_w, gate_decay_b, gate_input_b, decay_codes
-):
-    rows_here, channels = lru_in.shape
+def recurrence_inputs(rows_here, segment_ids, gate_decay_b, gate_input_b, decay_codes):
     ctx_index = lax.axis_index("ctx")
-    rim_rows = shifted_2(lru_in[rows_here - HALO :], "ctx", 1)
-    extended = jnp.concatenate([rim_rows, lru_in], axis=0)
     pad_seg = jnp.concatenate([jnp.full((CONV - 1,), -1, jnp.int32), segment_ids])
     ext_seg = lax.dynamic_slice_in_dim(pad_seg, ctx_index * rows_here, rows_here + CONV - 1)
     query_seg = ext_seg[CONV - 1 :]
@@ -180,6 +176,17 @@
         jnp.where(decay_codes[:, None] == levels[None, :], decay_rates()[None, :], 0.0), axis=1
     )
     vectors = jnp.stack([gate_decay_b, gate_input_b, decay_rate])
+    return flags, vectors, query_seg
+
+
+def recurrence(
+    lru_in, segment_ids, conv_weight, gate_decay_w, gate_input_w, gate_decay_b, gate_input_b, decay_codes
+):
+    rows_here, channels = lru_in.shape
+    ctx_index = lax.axis_index("ctx")
+    rim_rows = shifted_2(lru_in[rows_here - HALO :], "ctx", 1)
+    extended = jnp.concatenate([rim_rows, lru_in], axis=0)
+    flags, vectors, _ = recurrence_inputs(rows_here, segment_ids, gate_decay_b, gate_input_b, decay_codes)
     full = jax.ShapeDtypeStruct((rows_here, channels), jnp.float32)
     cum_keep, local_state = pl.pallas_call(
         scan_kernel,
@@ -197,6 +204,229 @@
     return states.astype(jnp.bfloat16)
 
 
+def fused_kernel(
+    blocks, members, q_ref, kv_ref, qseg_ref, kseg_ref, res_ref, ow_ref, lw_ref, gain_ref, flags_ref,
+    conv_ref, wd_ref, wi_ref, vec_ref, resid_ref, lru_ref,
+    kv_all, att, heads, sums, gained, partial, mixed, resid_in, resid_rows, inverse, ext, rim, ends, keep, state,
+    kv_z, kv_x, att_s, res_s, sum_s, gain_s, row_s, mix_s, inv_s, rim_s, end_s,
+):
+    group, c, m = lax.axis_index("groups"), lax.axis_index("ctx"), lax.axis_index("mp")
+    rows, cols = q_ref.shape
+    piece = rows // members
+    width = ow_ref.shape[1]
+
+    def ahead(offset):
+        return lax.rem(c + offset, blocks)
+
+    def behind(offset):
+        return lax.rem(c + blocks - offset, blocks)
+
+    def member(offset):
+        return lax.rem(m + offset, members)
+
+    def rows_of(which):
+        return pl.ds(pl.multiple_of(which * piece, piece), piece)
+
+    def cols_of(which):
+        return pl.ds(pl.multiple_of(which * width, width), width)
+
+    def send(src, dst, sems, index, to_c, to_m):
+        return pltpu.make_async_remote_copy(
+            src_ref=src, dst_ref=dst, send_sem=sems.at[(0, *index)], recv_sem=sems.at[(1, *index)],
+            device_id=(group, to_c, to_m), device_id_type=pl.DeviceIdType.MESH,
+        )
+
+    def kv_z_copy(i):
+        slot = kv_all.at[c * members + m]
+        return send(kv_ref, slot, kv_z, (i,), ahead(i), m)
+
+    def kv_x_copy(i, j):
+        slot = kv_all.at[behind(i) * members + m]
+        return send(slot, slot, kv_x, (i, j), c, member(j))
+
+    def res_copy(i):
+        return send(res_ref.at[:, cols_of(behind(i))], resid_in.at[i], res_s, (i,), behind(i), m)
+
+    def att_copy(i):
+        return send(att.at[0], att.at[i], att_s, (i,), behind(i), m)
+
+    def sum_copy(i, j):
+        return send(heads.at[i, rows_of(member(j))], sums.at[i, m], sum_s, (i, j), c, member(j))
+
+    def gain_copy(i, j):
+        return send(gained.at[i, rows_of(m)], gained.at[i, rows_of(m)], gain_s, (i, j), c, member(j))
+
+    def row_copy(i):
+        return send(resid_in.at[i], resid_rows.at[c], row_s, (i,), ahead(i), m)
+
+    def mix_copy(i):
+        return send(partial.at[i], mixed.at[i], mix_s, (i,), ahead(i), m)
+
+    def inv_copy(j):
+        return send(inverse.at[m], inverse.at[m], inv_s, (j,), c, member(j))
+
+    def rim_copy():
+        return send(ext.at[pl.ds(rows, HALO)], rim, rim_s, (0,), ahead(1), m)
+
+    def end_copy(i):
+        return send(ends.at[c], ends.at[c], end_s, (i,), ahead(i), m)
+
+    barrier = pltpu.get_barrier_semaphore()
+    for i in range(blocks):
+        for j in range(members):
+            if i or j:
+                pl.semaphore_signal(
+                    barrier, inc=1, device_id=(group, ahead(i), member(j)), device_id_type=pl.DeviceIdType.MESH
+                )
+    pl.semaphore_wait(barrier, blocks * members - 1)
+
+    kv_all[c * members + m] = kv_ref[...]
+    for i in range(1, blocks):
+        kv_z_copy(i).start()
+    for j in range(1, members):
+        kv_x_copy(0, j).start()
+    for i in range(1, blocks):
+        res_copy(i).start()
+    resid_in[0] = res_ref[:, cols_of(c)]
+    for i in range(1, blocks):
+        kv_z_copy(i).wait_recv()
+        for j in range(1, members):
+            kv_x_copy(i, j).start()
+    for i in range(blocks):
+        for j in range(1, members):
+            kv_x_copy(i, j).wait_recv()
+
+    tokens = kseg_ref.shape[1]
+    distance = (
+        c * rows
+        + lax.broadcasted_iota(jnp.int32, (rows, tokens), 0)
+        - lax.broadcasted_iota(jnp.int32, (rows, tokens), 1)
+    )
+    allowed = (distance >= 0) & (distance < WIN) & (qseg_ref[...] == kseg_ref[...])
+    keys_all = kv_all[...].reshape(tokens, 2 * HD)
+    for head in range(cols // HD):
+        span = slice(head * HD, (head + 1) * HD)
+        scores = lax.dot_general(
+            q_ref[:, span], keys_all[:, :HD], (((1,), (1,)), ((), ())), preferred_element_type=jnp.float32
+        ) * (1.0 / math.sqrt(HD))
+        scores = jnp.where(allowed, scores, -1e30)
+        weights = jnp.exp(scores - jnp.max(scores, axis=-1, keepdims=True))
+        probs = (weights / jnp.sum(weights, axis=-1, keepdims=True)).astype(jnp.bfloat16)
+        att[0, :, span] = jnp.dot(probs, keys_all[:, HD:], preferred_element_type=jnp.float32).astype(jnp.bfloat16)
+    for i in range(1, blocks):
+        att_copy(i).start()
+
+    tile = math.gcd(width, 256)
+
+    def multiply(source, weight, target, i):
+        @pl.loop(0, weight.shape[1] // tile)
+        def _(n):
+            span = pl.ds(pl.multiple_of(n * tile, tile), tile)
+            target[i, :, span] = jnp.dot(
+                source[i], weight[:, span], preferred_element_type=jnp.float32
+            ).astype(jnp.bfloat16)
+
+    @pl.loop(0, blocks + 2)
+    def _(tick):
+        @pl.when(tick < blocks)
+        def _():
+            @pl.when(tick > 0)
+            def _():
+                att_copy(tick).wait_recv()
+
+            multiply(att, ow_ref, heads, tick)
+            for j in range(1, members):
+                sum_copy(tick, j).start()
+
+        @pl.when((tick > 0) & (tick < blocks + 1))
+        def _():
+            i = tick - 1
+            sums[i, m] = heads[i, rows_of(m)]
+
+            @pl.when(i > 0)
+            def _():
+                res_copy(i).wait_recv()
+
+            total = resid_in[i].astype(jnp.float32)
+            for j in range(1, members):
+                sum_copy(i, j).wait_recv()
+            for j in range(members):
+                total = total + sums[i, j].astype(jnp.float32)
+            resid = total.astype(jnp.bfloat16)
+            gained[i, rows_of(m)] = (resid.astype(jnp.float32) * gain_ref[...]).astype(jnp.bfloat16)
+            for j in range(1, members):
+                gain_copy(i, j).start()
+            resid_in[i] = resid
+
+            @pl.when(i > 0)
+            def _():
+                row_copy(i).start()
+
+        @pl.when(tick > 1)
+        def _():
+            i = tick - 2
+            for j in range(1, members):
+                gain_copy(i, j).wait_recv()
+            multiply(gained, lw_ref, partial, i)
+
+            @pl.when(i > 0)
+            def _():
+                mix_copy(i).start()
+
+    resid_rows[c] = resid_in[0]
+    for i in range(1, blocks):
+        row_copy(i).wait_recv()
+    squares = jnp.zeros((piece, 1), jnp.float32)
+    for k in range(blocks):
+        resid = resid_rows[k]
+        resid_ref[:, k * width : (k + 1) * width] = resid
+        resid_f32 = resid.astype(jnp.float32)
+        squares = squares + jnp.sum(resid_f32 * resid_f32, axis=-1, keepdims=True)
+    inverse[m] = jnp.broadcast_to(lax.rsqrt(squares / (blocks * width) + 1e-06), inverse.shape[1:])
+    for j in range(1, members):
+        inv_copy(j).start()
+    for i in range(1, blocks):
+        mix_copy(i).wait_recv()
+    for j in range(1, members):
+        inv_copy(j).wait_recv()
+    scale = inverse[...].reshape(rows, inverse.shape[2])[:, 0:1]
+    total = partial[0].astype(jnp.float32)
+    for i in range(1, blocks):
+        total = total + mixed[i].astype(jnp.float32)
+    ext[HALO:] = (total * scale).astype(jnp.bfloat16)
+    rim_copy().start()
+    rim_copy().wait()
+    ext[:HALO] = rim[...]
+
+    scan_kernel(ext, flags_ref, conv_ref, wd_ref, wi_ref, vec_ref, keep, state)
+
+    ends[c, 0:8] = keep[rows - 8 :]
+    ends[c, 8:16] = state[rows - 8 :]
+    for i in range(1, blocks):
+        end_copy(i).start()
+    for i in range(1, blocks):
+        end_copy(i).wait_recv()
+    incoming = jnp.zeros((1, keep.shape[1]), jnp.float32)
+    for source in range(blocks - 1):
+        incoming = jnp.where(source < c, ends[source, 7:8] * incoming + ends[source, 15:16], incoming)
+    lru_ref[...] = (state[...] + keep[...] * incoming).astype(jnp.bfloat16)
+
+    for j in range(1, members):
+        inv_copy(j).wait_send()
+    for i in range(blocks):
+        for j in range(1, members):
+            kv_x_copy(i, j).wait_send()
+            sum_copy(i, j).wait_send()
+            gain_copy(i, j).wait_send()
+        if i:
+            kv_z_copy(i).wait_send()
+            res_copy(i).wait_send()
+            att_copy(i).wait_send()
+            row_copy(i).wait_send()
+            mix_copy(i).wait_send()
+            end_copy(i).wait_send()
+
+
 def local_stationary(
     queries,
     keyvals,
@@ -212,43 +442,46 @@
     decay_codes,
     norm_gain,
 ):
-    rows_here = queries.shape[0]
-    tokens = segment_ids.shape[0]
+    rows, cols = queries.shape
+    blocks, members = lax.axis_size("ctx"), lax.axis_size("mp")
+    piece = rows // members
+    width, channels = out_weight.shape[1], lru_weight.shape[1]
     ctx_index = lax.axis_index("ctx")
-    blocks, members = lax.axis_size("ctx"), lax.axis_size("mp")
-    piece = rows_here // members
-    cols = out_weight.shape[1]
-    keys_all = lax.all_gather(keyvals, ("ctx", "mp"), axis=0, tiled=True)
-    residual_cols = lax.all_to_all(residual, "ctx", split_axis=1, concat_axis=0, tiled=True)
-    query_seg = lax.dynamic_slice_in_dim(segment_ids, ctx_index * rows_here, rows_here)
-    query_pos = ctx_index * rows_here + jnp.arange(rows_here, dtype=jnp.int32)
-    distance = query_pos[:, None] - jnp.arange(tokens, dtype=jnp.int32)[None, :]
-    allowed = (distance >= 0) & (distance < WIN) & (query_seg[:, None] == segment_ids[None, :])
-    attended = attend_local(queries, keys_all, allowed)
-    attended_all = lax.all_gather(attended, "ctx", axis=0, tiled=True)
-    head_part = jnp.dot(attended_all, out_weight, preferred_element_type=jnp.float32)
-    summed = lax.psum_scatter(
-        head_part.astype(jnp.bfloat16).reshape(blocks, rows_here, cols), "mp", scatter_dimension=1, tiled=True
-    )
-    resid_cols = (
-        summed.reshape(blocks * piece, cols).astype(jnp.float32) + residual_cols.astype(jnp.float32)
-    ).astype(jnp.bfloat16)
-    resid_out = lax.all_to_all(resid_cols, "ctx", split_axis=0, concat_axis=1, tiled=True)
-    resid_f32 = resid_cols.astype(jnp.float32)
-    squares = jnp.sum(resid_f32 * resid_f32, axis=-1).reshape(blocks, piece)
-    all_squares = lax.all_gather(squares, ("ctx", "mp"), axis=0).reshape(blocks, members, blocks, piece)
-    own_squares = lax.dynamic_index_in_dim(all_squares, ctx_index, 2, keepdims=False)
-    mean_square = jnp.sum(own_squares, axis=0).reshape(rows_here) / residual.shape[1]
-    inverse = lax.rsqrt(mean_square + 1e-06)
-    gain = lax.dynamic_slice_in_dim(norm_gain, ctx_index * cols, cols)
-    gained = (resid_f32 * gain).astype(jnp.bfloat16).reshape(blocks, piece, cols)
-    gained_all = lax.all_gather(gained, "mp", axis=1, tiled=True).reshape(tokens, cols)
-    partial = jnp.dot(gained_all, lru_weight, preferred_element_type=jnp.float32).astype(jnp.bfloat16)
-    mixed = lax.psum_scatter(partial, "ctx", scatter_dimension=0, tiled=True)
-    lru_in = (mixed.astype(jnp.float32) * inverse[:, None]).astype(jnp.bfloat16)
-    return resid_out, recurrence(
-        lru_in, segment_ids, conv_weight, gate_decay_w, gate_input_w,
-        gate_decay_b, gate_input_b, decay_codes,
+    flags, vectors, query_seg = recurrence_inputs(rows, segment_ids, gate_decay_b, gate_input_b, decay_codes)
+    gain = lax.dynamic_slice_in_dim(norm_gain, ctx_index * width, width)[None]
+    bf16, f32 = jnp.bfloat16, jnp.float32
+    vmem = pl.BlockSpec(memory_space=pltpu.VMEM)
+    sems = [(blocks,), (blocks, members), (blocks,), (blocks,), (blocks, members), (blocks, members)]
+    sems = sems + [(blocks,), (blocks,), (members,), (1,), (blocks,)]
+    return pl.pallas_call(
+        functools.partial(fused_kernel, blocks, members),
+        out_shape=(jax.ShapeDtypeStruct(residual.shape, bf16), jax.ShapeDtypeStruct((rows, channels), bf16)),
+        in_specs=[vmem] * 13,
+        out_specs=(vmem, vmem),
+        scratch_shapes=[
+            pltpu.VMEM((blocks * members,) + keyvals.shape, bf16),
+            pltpu.VMEM((blocks, rows, cols), bf16),
+            pltpu.VMEM((blocks, rows, width), bf16),
+            pltpu.VMEM((blocks, members, piece, width), bf16),
+            pltpu.VMEM((blocks, rows, width), bf16),
+            pltpu.VMEM((blocks, rows, channels), bf16),
+            pltpu.VMEM((blocks, rows, channels), bf16),
+            pltpu.VMEM((blocks, piece, width), bf16),
+            pltpu.VMEM((blocks, piece, width), bf16),
+            pltpu.VMEM((members, piece, 128), f32),
+            pltpu.VMEM((rows + HALO, channels), bf16),
+            pltpu.VMEM((HALO, channels), bf16),
+            pltpu.VMEM((blocks, 16, channels), f32),
+            pltpu.VMEM((rows, channels), f32),
+            pltpu.VMEM((rows, channels), f32),
+        ]
+        + [pltpu.SemaphoreType.DMA((2,) + shape) for shape in sems],
+        compiler_params=pltpu.CompilerParams(
+            collective_id=0, has_side_effects=True, vmem_limit_bytes=56 * 1024 * 1024
+        ),
+    )(
+        queries, keyvals, query_seg[:, None], segment_ids[None], residual, out_weight, lru_weight, gain,
+        flags, conv_weight, gate_decay_w, gate_input_w, vectors,
     )
 
 

time: 256 us -> 155 us (0.61)
  waiting for transfers between devices: 146 us -> 0 us
  Pallas kernels: 3.09 us -> 144 us
  blocking collectives: 46.8 us -> 0 us
  matrix products: 14.7 us -> 0 us
  starting transfers between devices: 13.7 us -> 0 us
  between operations: 14 us -> 0.67 us
  other arithmetic: 8.9 us -> 2.19 us
    pallas_call x1, Pallas kernels: 3.09 us -> 144 us  [local_stationary(): pl.pallas_call(functools.partial(fused_kernel, blocks, members), out_shap...]
    all_gather x3 -> x0, waiting for transfers between devices: 109 us -> none  [the longest x1 45.3 us: local_stationary(): attended_all = lax.all_gather(attended, 'ctx', axis=0, tiled=True)]
    all_gather x2 -> x0, blocking collectives: 46.8 us -> none  [the longest x1 33.7 us: local_stationary(): lax.all_gather(squares, ('ctx', 'mp'), axis=0)]
    reduce_scatter x2 -> x0, waiting for transfers between devices: 23.3 us -> none  [the longest x1 12.8 us: local_stationary(): mixed = lax.psum_scatter(partial, 'ctx', scatter_dimension=0, tiled=True)]
    dot_general x4 -> x0, matrix products: 14.7 us -> none  [the longest x1 5.88 us: local_stationary(): jnp.dot(gained_all, lru_weight, preferred_element_type=jnp.float32)]
    all_to_all x2 -> x0, waiting for transfers between devices: 13.3 us -> none  [the longest x1 13.3 us: local_stationary(): lax.all_to_all(residual, 'ctx', split_axis=1, concat_axis=0, tiled=True)]
    all_to_all x2 -> x0, starting transfers between devices: 8.21 us -> none  [the longest x1 4.74 us: local_stationary(): lax.all_to_all(resid_cols, 'ctx', split_axis=0, concat_axis=1, tiled=True)]
    ppermute x1 -> x0, starting transfers between devices: 5.28 us -> none  [shifted_2(): lax.ppermute(value, axis, [(source, source + steps) for source in range(i...]
  transfers between devices with their start and end apart: 8 -> 0, of which waited for: 6 -> 0; matrix products, arithmetic and copies ran while one was open for 3% -> 0% of each run, Pallas kernels for 0% -> 0%
where the time goes in v2:
time: 155 us; the launch traced here: 154 us
  Pallas kernels  144 us (93%)
  local copies, waits for them, and re-layouts  7.49 us (5%)
  other arithmetic  2.19 us (1%)
    pallas_call x1, Pallas kernels, local_stationary(): pl.pallas_call(functools.partial(fused_kernel, blocks, members), out_shap...  144 us
    unnamed x2, local copies, waits for them, and re-layouts  3.74 us

profile of v2, /device:TPU:0, one launch (start us, length us, event | category | flops | bytes accessed | tf_op | source)
XLA Modules:
  0.0 154.5 jit_solution(8184477028229740131)
XLA Ops:
  0.6 0.8 pad_dynamic-slice_fusion
  1.4 0.1 slice.12
  1.5 0.1 fusion
  1.6 0.8 select_reduce_fusion
  2.4 1.3 dynamic_slice.7
  3.7 1.3 pad_maximum_fusion.vec_ref
  5.0 0.8 copy.25.flags_ref
  5.8 0.8 copy.24.qseg_ref
  6.6 144.1 %shard_map.140 = (bf16[64,4096]{1,0:T(8,128)(2,1)}, bf16[256,1024]{1,0:T(8,128)(2,1)}) custom-call(bf16[256,1024]{1,0:T(8,128)(2,1)} %q_ref.1, bf16[64,512]{1,0:T(8,128)(2,1)} %kv_ref.1, s32[256,1]{1,0:T(8,128)} %copy.24.qseg_ref, s32[1,1024]{1,0:T(1,128)} %bitcast.7, bf16[64,4096]{1,0:T(8,128)(2,1)} %res_ref.1, bf16[1024,1024]{1,0:T(8,128)(2,1)} %ow_ref.1, ...), custom_call_target="tpu_custom_call" | custom-call | tf_op jit(solution)/shard_map/pallas_call | solution.py:456
  150.7 1.9 %copy.28 = bf16[64,4096]{1,0:T(8,128)(2,1)} copy(bf16[64,4096]{1,0:T(8,128)(2,1)} %get-tuple-element.8) | data formatting | bytes 1048576
  152.6 1.9 %copy.29 = bf16[256,1024]{1,0:T(8,128)(2,1)} copy(bf16[256,1024]{1,0:T(8,128)(2,1)} %get-tuple-element.9) | data formatting | bytes 1048576
  (6 shorter events, 0.1 us)

commit v3 on v2

--- a/solution.py
+++ b/solution.py
@@ -230,9 +230,10 @@
     def cols_of(which):
         return pl.ds(pl.multiple_of(which * width, width), width)
 
-    def send(src, dst, sems, index, to_c, to_m):
+    def send(src, dst, sems, index, to_c, to_m, landing=None):
+        landing = index if landing is None else landing
         return pltpu.make_async_remote_copy(
-            src_ref=src, dst_ref=dst, send_sem=sems.at[(0, *index)], recv_sem=sems.at[(1, *index)],
+            src_ref=src, dst_ref=dst, send_sem=sems.at[(0, *index)], recv_sem=sems.at[(1, *landing)],
             device_id=(group, to_c, to_m), device_id_type=pl.DeviceIdType.MESH,
         )
 
@@ -245,10 +246,33 @@
         return send(slot, slot, kv_x, (i, j), c, member(j))
 
     def res_copy(i):
-        return send(res_ref.at[:, cols_of(behind(i))], resid_in.at[i], res_s, (i,), behind(i), m)
-
-    def att_copy(i):
-        return send(att.at[0], att.at[i], att_s, (i,), behind(i), m)
+        return send(res_ref.at[:, cols_of(ahead(i))], resid_in.at[c], res_s, (i,), ahead(i), m, (c,))
+
+    def res_arrival(b):
+        return send(res_ref.at[:, cols_of(c)], resid_in.at[b], res_s, (0,), b, m, (b,))
+
+    def att_right(b):
+        return send(att.at[b], att.at[b], att_s, (b,), ahead(1), m)
+
+    def att_left(b):
+        return send(att.at[b], att.at[b], att_s, (b + blocks,), behind(1), m, (b,))
+
+    def relay(b, act):
+        @pl.when((b <= c) & (c < blocks - 1))
+        def _():
+            act(att_right(b))
+
+        @pl.when((b >= c) & (c > 0))
+        def _():
+            act(att_left(b))
+
+    nearer = jnp.minimum(c, blocks - 1 - c)
+
+    def block_at(tick):
+        both = tick <= 2 * nearer
+        steps = jnp.where(both, lax.div(tick + 1, 2), tick - nearer)
+        leftward = jnp.where(both, lax.rem(tick, 2) == 1, c > nearer)
+        return jnp.where(leftward, c - steps, c + steps)
 
     def sum_copy(i, j):
         return send(heads.at[i, rows_of(member(j))], sums.at[i, m], sum_s, (i, j), c, member(j))
@@ -256,11 +280,17 @@
     def gain_copy(i, j):
         return send(gained.at[i, rows_of(m)], gained.at[i, rows_of(m)], gain_s, (i, j), c, member(j))
 
-    def row_copy(i):
-        return send(resid_in.at[i], resid_rows.at[c], row_s, (i,), ahead(i), m)
-
-    def mix_copy(i):
-        return send(partial.at[i], mixed.at[i], mix_s, (i,), ahead(i), m)
+    def row_copy(b):
+        return send(resid_in.at[b], resid_rows.at[c], row_s, (b,), b, m, (c,))
+
+    def mix_copy(i, b):
+        return send(partial.at[i], mixed.at[c], mix_s, (b,), b, m, (c,))
+
+    def row_arrival(i):
+        return send(resid_in.at[0], resid_rows.at[c], row_s, (0,), ahead(i), m, (ahead(i),))
+
+    def mix_arrival(i):
+        return send(partial.at[0], mixed.at[c], mix_s, (0,), ahead(i), m, (ahead(i),))
 
     def inv_copy(j):
         return send(inverse.at[m], inverse.at[m], inv_s, (j,), c, member(j))
@@ -287,7 +317,7 @@
         kv_x_copy(0, j).start()
     for i in range(1, blocks):
         res_copy(i).start()
-    resid_in[0] = res_ref[:, cols_of(c)]
+    resid_in[c] = res_ref[:, cols_of(c)]
     for i in range(1, blocks):
         kv_z_copy(i).wait_recv()
         for j in range(1, members):
@@ -312,42 +342,45 @@
         scores = jnp.where(allowed, scores, -1e30)
         weights = jnp.exp(scores - jnp.max(scores, axis=-1, keepdims=True))
         probs = (weights / jnp.sum(weights, axis=-1, keepdims=True)).astype(jnp.bfloat16)
-        att[0, :, span] = jnp.dot(probs, keys_all[:, HD:], preferred_element_type=jnp.float32).astype(jnp.bfloat16)
-    for i in range(1, blocks):
-        att_copy(i).start()
+        att[c, :, span] = jnp.dot(probs, keys_all[:, HD:], preferred_element_type=jnp.float32).astype(jnp.bfloat16)
+    relay(c, lambda copy: copy.start())
 
     tile = math.gcd(width, 256)
 
-    def multiply(source, weight, target, i):
+    def multiply(source, at, weight, target, i):
         @pl.loop(0, weight.shape[1] // tile)
         def _(n):
             span = pl.ds(pl.multiple_of(n * tile, tile), tile)
             target[i, :, span] = jnp.dot(
-                source[i], weight[:, span], preferred_element_type=jnp.float32
+                source[at], weight[:, span], preferred_element_type=jnp.float32
             ).astype(jnp.bfloat16)
 
     @pl.loop(0, blocks + 2)
     def _(tick):
         @pl.when(tick < blocks)
         def _():
+            b = block_at(tick)
+
             @pl.when(tick > 0)
             def _():
-                att_copy(tick).wait_recv()
-
-            multiply(att, ow_ref, heads, tick)
+                att_right(b).wait_recv()
+                relay(b, lambda copy: copy.start())
+
+            multiply(att, b, ow_ref, heads, tick)
             for j in range(1, members):
                 sum_copy(tick, j).start()
 
         @pl.when((tick > 0) & (tick < blocks + 1))
         def _():
             i = tick - 1
+            b = block_at(i)
             sums[i, m] = heads[i, rows_of(m)]
 
             @pl.when(i > 0)
             def _():
-                res_copy(i).wait_recv()
-
-            total = resid_in[i].astype(jnp.float32)
+                res_arrival(b).wait_recv()
+
+            total = resid_in[b].astype(jnp.float32)
             for j in range(1, members):
                 sum_copy(i, j).wait_recv()
             for j in range(members):
@@ -356,26 +389,26 @@
             gained[i, rows_of(m)] = (resid.astype(jnp.float32) * gain_ref[...]).astype(jnp.bfloat16)
             for j in range(1, members):
                 gain_copy(i, j).start()
-            resid_in[i] = resid
+            resid_in[b] = resid
 
             @pl.when(i > 0)
             def _():
-                row_copy(i).start()
+                row_copy(b).start()
 
         @pl.when(tick > 1)
         def _():
             i = tick - 2
             for j in range(1, members):
                 gain_copy(i, j).wait_recv()
-            multiply(gained, lw_ref, partial, i)
+            multiply(gained, i, lw_ref, partial, i)
 
             @pl.when(i > 0)
             def _():
-                mix_copy(i).start()
-
-    resid_rows[c] = resid_in[0]
-    for i in range(1, blocks):
-        row_copy(i).wait_recv()
+                mix_copy(i, block_at(i)).start()
+
+    resid_rows[c] = resid_in[c]
+    for i in range(1, blocks):
+        row_arrival(i).wait_recv()
     squares = jnp.zeros((piece, 1), jnp.float32)
     for k in range(blocks):
         resid = resid_rows[k]
@@ -386,13 +419,14 @@
     for j in range(1, members):
         inv_copy(j).start()
     for i in range(1, blocks):
-        mix_copy(i).wait_recv()
+        mix_arrival(i).wait_recv()
     for j in range(1, members):
         inv_copy(j).wait_recv()
     scale = inverse[...].reshape(rows, inverse.shape[2])[:, 0:1]
-    total = partial[0].astype(jnp.float32)
-    for i in range(1, blocks):
-        total = total + mixed[i].astype(jnp.float32)
+    mixed[c] = partial[0]
+    total = mixed[0].astype(jnp.float32)
+    for k in range(1, blocks):
+        total = total + mixed[k].astype(jnp.float32)
     ext[HALO:] = (total * scale).astype(jnp.bfloat16)
     rim_copy().start()
     rim_copy().wait()
@@ -418,12 +452,12 @@
             kv_x_copy(i, j).wait_send()
             sum_copy(i, j).wait_send()
             gain_copy(i, j).wait_send()
+        relay(block_at(i), lambda copy: copy.wait_send())
         if i:
             kv_z_copy(i).wait_send()
             res_copy(i).wait_send()
-            att_copy(i).wait_send()
-            row_copy(i).wait_send()
-            mix_copy(i).wait_send()
+            row_copy(block_at(i)).wait_send()
+            mix_copy(i, block_at(i)).wait_send()
             end_copy(i).wait_send()
 
 
@@ -451,7 +485,7 @@
     gain = lax.dynamic_slice_in_dim(norm_gain, ctx_index * width, width)[None]
     bf16, f32 = jnp.bfloat16, jnp.float32
     vmem = pl.BlockSpec(memory_space=pltpu.VMEM)
-    sems = [(blocks,), (blocks, members), (blocks,), (blocks,), (blocks, members), (blocks, members)]
+    sems = [(blocks,), (blocks, members), (2 * blocks,), (blocks,), (blocks, members), (blocks, members)]
     sems = sems + [(blocks,), (blocks,), (members,), (1,), (blocks,)]
     return pl.pallas_call(
         functools.partial(fused_kernel, blocks, members),

time: 155 us -> 151 us (0.974)
  Pallas kernels: 144 us -> 139 us
    pallas_call x1, Pallas kernels: 144 us -> 139 us  [local_stationary(): pl.pallas_call(functools.partial(fused_kernel, blocks, members), out_shap...]
where the time goes in v3:
time: 151 us; the launch traced here: 150 us
  Pallas kernels  139 us (92%)
  local copies, waits for them, and re-layouts  7.49 us (5%)
  other arithmetic  2.19 us (1%)
    pallas_call x1, Pallas kernels, local_stationary(): pl.pallas_call(functools.partial(fused_kernel, blocks, members), out_shap...  139 us
    unnamed x2, local copies, waits for them, and re-layouts  3.74 us

profile of v3, /device:TPU:0, one launch (start us, length us, event | category | flops | bytes accessed | tf_op | source)
XLA Modules:
  0.0 149.7 jit_solution(610084917742094706)
XLA Ops:
  0.6 0.8 pad_dynamic-slice_fusion
  1.4 0.1 slice.12
  1.5 0.1 fusion
  1.6 0.8 select_reduce_fusion
  2.4 1.3 dynamic_slice.7
  3.7 1.3 pad_maximum_fusion.vec_ref
  5.0 0.8 copy.25.flags_ref
  5.8 0.8 copy.24.qseg_ref
  6.6 139.3 %shard_map.140 = (bf16[64,4096]{1,0:T(8,128)(2,1)}, bf16[256,1024]{1,0:T(8,128)(2,1)}) custom-call(bf16[256,1024]{1,0:T(8,128)(2,1)} %q_ref.1, bf16[64,512]{1,0:T(8,128)(2,1)} %kv_ref.1, s32[256,1]{1,0:T(8,128)} %copy.24.qseg_ref, s32[1,1024]{1,0:T(1,128)} %bitcast.7, bf16[64,4096]{1,0:T(8,128)(2,1)} %res_ref.1, bf16[1024,1024]{1,0:T(8,128)(2,1)} %ow_ref.1, ...), custom_call_target="tpu_custom_call" | custom-call | tf_op jit(solution)/shard_map/pallas_call | solution.py:490
  145.9 1.9 %copy.28 = bf16[64,4096]{1,0:T(8,128)(2,1)} copy(bf16[64,4096]{1,0:T(8,128)(2,1)} %get-tuple-element.8) | data formatting | bytes 1048576
  147.8 1.9 %copy.29 = bf16[256,1024]{1,0:T(8,128)(2,1)} copy(bf16[256,1024]{1,0:T(8,128)(2,1)} %get-tuple-element.9) | data formatting | bytes 1048576
  (6 shorter events, 0.1 us)

commit v4 on v3

--- a/solution.py
+++ b/solution.py
@@ -251,20 +251,20 @@
     def res_arrival(b):
         return send(res_ref.at[:, cols_of(c)], resid_in.at[b], res_s, (0,), b, m, (b,))
 
-    def att_right(b):
-        return send(att.at[b], att.at[b], att_s, (b,), ahead(1), m)
-
-    def att_left(b):
-        return send(att.at[b], att.at[b], att_s, (b + blocks,), behind(1), m, (b,))
-
-    def relay(b, act):
+    def att_right(b, span=slice(None)):
+        return send(att.at[b, :, span], att.at[b, :, span], att_s, (b,), ahead(1), m)
+
+    def att_left(b, span=slice(None)):
+        return send(att.at[b, :, span], att.at[b, :, span], att_s, (b + blocks,), behind(1), m, (b,))
+
+    def relay(b, act, span=slice(None)):
         @pl.when((b <= c) & (c < blocks - 1))
         def _():
-            act(att_right(b))
+            act(att_right(b, span))
 
         @pl.when((b >= c) & (c > 0))
         def _():
-            act(att_left(b))
+            act(att_left(b, span))
 
     nearer = jnp.minimum(c, blocks - 1 - c)
 
@@ -343,7 +343,7 @@
         weights = jnp.exp(scores - jnp.max(scores, axis=-1, keepdims=True))
         probs = (weights / jnp.sum(weights, axis=-1, keepdims=True)).astype(jnp.bfloat16)
         att[c, :, span] = jnp.dot(probs, keys_all[:, HD:], preferred_element_type=jnp.float32).astype(jnp.bfloat16)
-    relay(c, lambda copy: copy.start())
+        relay(c, lambda copy: copy.start(), span)
 
     tile = math.gcd(width, 256)
 
@@ -386,7 +386,7 @@
             for j in range(members):
                 total = total + sums[i, j].astype(jnp.float32)
             resid = total.astype(jnp.bfloat16)
-            gained[i, rows_of(m)] = (resid.astype(jnp.float32) * gain_ref[...]).astype(jnp.bfloat16)
+            gained[i, rows_of(m)] = (resid.astype(jnp.float32) * gain_ref[:, cols_of(c)]).astype(jnp.bfloat16)
             for j in range(1, members):
                 gain_copy(i, j).start()
             resid_in[b] = resid
@@ -482,7 +482,7 @@
     width, channels = out_weight.shape[1], lru_weight.shape[1]
     ctx_index = lax.axis_index("ctx")
     flags, vectors, query_seg = recurrence_inputs(rows, segment_ids, gate_decay_b, gate_input_b, decay_codes)
-    gain = lax.dynamic_slice_in_dim(norm_gain, ctx_index * width, width)[None]
+    gain = norm_gain[None]
     bf16, f32 = jnp.bfloat16, jnp.float32
     vmem = pl.BlockSpec(memory_space=pltpu.VMEM)
     sems = [(blocks,), (blocks, members), (2 * blocks,), (blocks,), (blocks, members), (blocks, members)]

time: 151 us -> 148 us (0.980)
  no operation moved by 1% of the time
where the time goes in v4:
time: 148 us; the launch traced here: 147 us
  Pallas kernels  138 us (93%)
  local copies, waits for them, and re-layouts  6.21 us (4%)
  other arithmetic  2.19 us (1%)
    pallas_call x1, Pallas kernels, local_stationary(): pl.pallas_call(functools.partial(fused_kernel, blocks, members), out_shap...  138 us
    unnamed x2, local copies, waits for them, and re-layouts  3.74 us

profile of v4, /device:TPU:0, one launch (start us, length us, event | category | flops | bytes accessed | tf_op | source)
XLA Modules:
  0.0 147.2 jit_solution(8824706465429435812)
XLA Ops:
  0.6 0.8 pad_dynamic-slice_fusion
  1.4 0.1 slice.12
  1.5 0.1 fusion
  1.6 0.8 select_reduce_fusion
  2.4 1.3 pad_maximum_fusion.vec_ref
  3.7 0.8 copy.25.flags_ref
  4.5 0.8 copy.24.qseg_ref
  5.3 138.1 %shard_map.140 = (bf16[64,4096]{1,0:T(8,128)(2,1)}, bf16[256,1024]{1,0:T(8,128)(2,1)}) custom-call(bf16[256,1024]{1,0:T(8,128)(2,1)} %q_ref.1, bf16[64,512]{1,0:T(8,128)(2,1)} %kv_ref.1, s32[256,1]{1,0:T(8,128)} %copy.24.qseg_ref, s32[1,1024]{1,0:T(1,128)} %bitcast.8, bf16[64,4096]{1,0:T(8,128)(2,1)} %res_ref.1, bf16[1024,1024]{1,0:T(8,128)(2,1)} %ow_ref.1, ...), custom_call_target="tpu_custom_call" | custom-call | tf_op jit(solution)/shard_map/pallas_call | solution.py:490
  143.5 1.9 %copy.28 = bf16[64,4096]{1,0:T(8,128)(2,1)} copy(bf16[64,4096]{1,0:T(8,128)(2,1)} %get-tuple-element.8) | data formatting | bytes 1048576
  145.3 1.9 %copy.29 = bf16[256,1024]{1,0:T(8,128)(2,1)} copy(bf16[256,1024]{1,0:T(8,128)(2,1)} %get-tuple-element.9) | data formatting | bytes 1048576
  (6 shorter events, 0.1 us)
